TPU v7x, 512 devices: a whole 4x4x16 slice. The times are simulated.
512 devices in a mesh: ep: 32 (over z, core), rep: 16 (over y, x).
Axes of the slice: x: 4, y: 4, z: 16, core: 2. Of those that a mesh axis runs over, the one named last changes fastest.
Arguments:
- frames: bfloat16 [65536, 1024], P(('ep', 'rep')), may hold values from -6 to 6
- lengths: int32 [512], P(('ep', 'rep')), may hold values from 64 to 128
- routes: int32 [65536, 2], P(('ep', 'rep')), may hold values from 0 to 31, all different within a row; in each aligned block of 128 rows (0 to 127, 128 to 255, ...) at most 8 rows name the same one
- gate_weights: float32 [65536, 2], P(('ep', 'rep')), may hold values from 0.25 to 1
- kernel: float32 [31, 1024], replicated, may hold values from -1 to 1
- up_weight: bfloat16 [32, 2048, 1024], P('ep', 'rep'), may hold values from -0.1875 to 0.1875
- down_weight: bfloat16 [32, 2048, 1024], P('ep', 'rep'), may hold values from -0.125 to 0.125
- cotangent: bfloat16 [65536, 1024], P(('ep', 'rep')), may hold values from -1.5 to 1.5
Outputs:
- block_out: bfloat16 [65536, 1024], P(('ep', 'rep'))
- frame_grad: bfloat16 [65536, 1024], P(('ep', 'rep'))
- up_grad: float32 [32, 2048, 1024], P('ep', 'rep')
- down_grad: float32 [32, 2048, 1024], P('ep', 'rep')
Inputs may be any that keep to these rules, and one draw needn't show every extreme that they name: The 128 frames of one utterance name every expert in exactly 8 of their routes; a frame's 2 experts differ.
All inputs are finite; a program needn't handle non-finite values.
Results may differ from a plain program's by a relative error of at most 0.015.
Values may be sent and summed in bfloat16 or wider, within the bound.
A program may use at most 128 MiB of HBM per device.

v0:
```python
import jax
import jax.numpy as jnp
from jax import lax
from jax.sharding import PartitionSpec as P

norm_eps = 1e-05


def normalize(values):
    center = values - jnp.mean(values, axis=-1, keepdims=True)
    inverse = lax.rsqrt(jnp.mean(center * center, axis=-1, keepdims=True) + norm_eps)
    return (center * inverse, inverse)


def norm_back(normed, inverse, upstream):
    mean_grad = jnp.mean(upstream, axis=-1, keepdims=True)
    mean_cross = jnp.mean(upstream * normed, axis=-1, keepdims=True)
    return inverse * (upstream - mean_grad - normed * mean_cross)


def silu_slope(values):
    sigmoid_part = jax.nn.sigmoid(values)
    return sigmoid_part + values * sigmoid_part * (1.0 - sigmoid_part)


def depthwise(values, kernel):
    kernel_width = kernel.shape[0]
    half_width = kernel_width // 2
    length_rows = values.shape[0]
    padded = jnp.pad(values, ((half_width, half_width), (0, 0)))
    summed = jnp.zeros_like(values)
    for offset in range(kernel_width):
        summed = summed + kernel[offset] * padded[offset : offset + length_rows]
    return summed


def depthwise_back(upstream, kernel):
    kernel_width = kernel.shape[0]
    half_width = kernel_width // 2
    length_rows = upstream.shape[0]
    padded = jnp.pad(upstream, ((half_width, half_width), (0, 0)))
    summed = jnp.zeros_like(upstream)
    for offset in range(kernel_width):
        start_row = 2 * half_width - offset
        summed = summed + kernel[offset] * padded[start_row : start_row + length_rows]
    return summed


def per_rep_sum(left_cols, right_rows, rep_count):
    count_rows = right_rows.shape[0] // rep_count
    partials = jnp.einsum(
        "rcw,rcd->rwd",
        left_cols.reshape(rep_count, count_rows, -1),
        right_rows.reshape(rep_count, count_rows, -1),
        preferred_element_type=jnp.float32,
    )
    partials = lax.optimization_barrier(partials.astype(jnp.bfloat16)).astype(jnp.float32)
    return jnp.sum(partials, axis=0)


def on_device(frames, lengths, routes, gate_weights, kernel, up_weight, down_weight, cotangent):
    frame_count = frames.shape[0]
    experts = lax.axis_size("ep")
    rep_count = lax.axis_size("rep")
    pair_count = routes.shape[0] * routes.shape[1]
    cap_rows = pair_count // experts
    positions = lax.broadcasted_iota(jnp.int32, (frame_count, 1), 0)
    live_mask = (positions < lengths[0]).astype(jnp.float32)
    frames_wide = frames.astype(jnp.float32)
    first_hat, first_inv = normalize(frames_wide)
    conv_pre = depthwise(first_hat * live_mask, kernel)
    residual = frames_wide + jax.nn.silu(conv_pre)
    second_hat, second_inv = normalize(residual)
    normed = second_hat.astype(jnp.bfloat16)
    live_gate = gate_weights * live_mask
    flat_routes = routes.reshape(pair_count)
    expert_ids = lax.broadcasted_iota(jnp.int32, (pair_count, experts), 1)
    one_hot = (flat_routes[:, None] == expert_ids).astype(jnp.bfloat16)
    row_ids = lax.broadcasted_iota(jnp.int32, (pair_count, pair_count), 0)
    col_ids = lax.broadcasted_iota(jnp.int32, (pair_count, pair_count), 1)
    earlier = (col_ids < row_ids).astype(jnp.bfloat16)
    before = jnp.dot(earlier, one_hot, preferred_element_type=jnp.float32)
    rank_of = jnp.sum(before * one_hot.astype(jnp.float32), axis=1).astype(jnp.int32)
    slot_of = flat_routes * cap_rows + rank_of
    placement = (row_ids == slot_of[None, :]).astype(jnp.bfloat16)
    frame_pick = jnp.sum(placement.reshape(pair_count, frame_count, -1), axis=2)
    cot_pairs = (live_gate[:, :, None] * cotangent.astype(jnp.float32)[:, None, :]).reshape(
        pair_count, -1
    )
    cot_pairs = cot_pairs.astype(jnp.bfloat16)
    send_rows = jnp.dot(frame_pick, normed, preferred_element_type=jnp.float32).astype(jnp.bfloat16)
    send_slopes = jnp.dot(placement, cot_pairs, preferred_element_type=jnp.float32).astype(
        jnp.bfloat16
    )
    recv_rows, recv_slopes = (
        lax.all_to_all(send_rows, "ep", split_axis=0, concat_axis=0, tiled=True),
        lax.all_to_all(send_slopes, "ep", split_axis=0, concat_axis=0, tiled=True),
    )
    up_local = up_weight[0]
    down_local = down_weight[0]
    up_all, down_all, rows_all = (
        lax.all_gather(up_local, "rep", axis=0, tiled=True),
        lax.all_gather(down_local, "rep", axis=0, tiled=True),
        lax.all_gather(recv_rows, "rep", axis=0, tiled=True),
    )
    contract = (((1,), (1,)), ((), ()))
    pre_hidden = lax.dot_general(recv_rows, up_all, contract, preferred_element_type=jnp.float32)
    hidden = jax.nn.silu(pre_hidden).astype(jnp.bfloat16)
    expert_out = jnp.dot(hidden, down_all, preferred_element_type=jnp.float32).astype(jnp.bfloat16)
    hidden_grad = lax.dot_general(
        recv_slopes, down_all, contract, preferred_element_type=jnp.float32
    )
    slopes = (hidden_grad * silu_slope(pre_hidden)).astype(jnp.bfloat16)
    row_grad = jnp.dot(slopes, up_all, preferred_element_type=jnp.float32).astype(jnp.bfloat16)
    back_out, back_grad = (
        lax.all_to_all(expert_out, "ep", split_axis=0, concat_axis=0, tiled=True),
        lax.all_to_all(row_grad, "ep", split_axis=0, concat_axis=0, tiled=True),
    )
    column_dims = (((0,), (0,)), ((), ()))
    slope_cols = lax.all_to_all(slopes, "rep", split_axis=1, concat_axis=0, tiled=True)
    up_grad = per_rep_sum(slope_cols, rows_all, rep_count)
    down_grad = lax.psum_scatter(
        lax.dot_general(
            hidden, recv_slopes, column_dims, preferred_element_type=jnp.float32
        ).astype(jnp.bfloat16),
        "rep",
        scatter_dimension=0,
        tiled=True,
    ).astype(jnp.float32)
    pair_out = lax.dot_general(placement, back_out, column_dims, preferred_element_type=jnp.float32)
    pair_out = pair_out.reshape(frame_count, -1, normed.shape[1])
    mixture = jnp.sum(live_gate[:, :, None] * pair_out, axis=1)
    block_out = (residual + mixture).astype(jnp.bfloat16)
    normed_grad = lax.dot_general(
        frame_pick, back_grad, column_dims, preferred_element_type=jnp.float32
    )
    residual_grad = cotangent.astype(jnp.float32) + norm_back(second_hat, second_inv, normed_grad)
    conv_grad = residual_grad * silu_slope(conv_pre)
    first_grad = depthwise_back(conv_grad, kernel) * live_mask
    frame_grad = (residual_grad + norm_back(first_hat, first_inv, first_grad)).astype(jnp.bfloat16)
    return (block_out, frame_grad, up_grad[None], down_grad[None])


def solution(mesh):
    in_specs = (
        P(("ep", "rep"), None),
        P(("ep", "rep")),
        P(("ep", "rep"), None),
        P(("ep", "rep"), None),
        P(),
        P("ep", "rep", None),
        P("ep", "rep", None),
        P(("ep", "rep"), None),
    )
    out_specs = (
        P(("ep", "rep"), None),
        P(("ep", "rep"), None),
        P("ep", "rep", None),
        P("ep", "rep", None),
    )
    return jax.shard_map(
        on_device, mesh=mesh, in_specs=in_specs, out_specs=out_specs, check_vma=False
    )
```

profile of v0, /device:TPU:1, one launch (start us, length us, event | category | flops | bytes accessed | tf_op | source)
XLA Modules:
  0.0 358.8 jit_solution(18225517476798386100)
XLA Ops:
  7.2 0.0 copy-start
  7.2 0.0 all-gather.8.cloned.1.call-start
  7.2 0.7 all-gather.8.cloned.1.call-update
  7.9 0.0 all-gather.10.cloned.1.call-start
  8.0 0.7 all-gather.10.cloned.1.call-update
  9.3 0.8 copy.27
  10.1 0.1 reshape.124
  10.2 0.2 fusion.31
  10.5 0.1 convert_element_type.87
  10.6 0.1 copy.28
  10.7 0.7 multiply_add_fusion.1
  11.4 1.1 convert_reduce_fusion.1
  12.5 1.2 fusion.43
  13.7 1.1 fusion.191
  14.8 1.2 fusion.190
  16.0 1.2 fusion.37
  17.2 0.0 copy-done
  17.2 0.0 copy-start.1
  17.2 3.0 fusion.188
  20.2 0.2 multiply_reduce_fusion.1
  20.4 1.2 fusion.23
  21.6 16.9 %all-to-all-start = ((bf16[32,8,1024]{2,1,0:T(8,128)(2,1)}), bf16[32,8,1024]{2,1,0:T(8,128)(2,1)}, u32[]{:S(2)}, u32[]{:S(2)}) async-start(bf16[32,8,1024]{2,1,0:T(8,128)(2,1)} %fusion.23), calls=%async_computation | async-start | bytes 1048576 | tf_op jit(solution)/shard_map/all_to_all | solution.py:96
  38.6 0.0 copy-done.1
  38.6 0.3 mul.754
  38.9 0.7 mul.755
  39.6 0.6 broadcast_multiply_fusion
  40.2 0.8 copy.30
  40.9 0.1 mul.752
  41.1 1.2 fusion.30
  42.3 29.9 %all-to-all-done = bf16[32,8,1024]{2,1,0:T(8,128)(2,1)} async-done(((bf16[32,8,1024]{2,1,0:T(8,128)(2,1)}), bf16[32,8,1024]{2,1,0:T(8,128)(2,1)}, u32[]{:S(2)}, u32[]{:S(2)}) %all-to-all-start) | async-done | bytes 524320 | tf_op jit(solution)/shard_map/all_to_all | solution.py:96
  72.1 4.0 %all-to-all-start.2 = ((bf16[32,8,1024]{2,1,0:T(8,128)(2,1)}), bf16[32,8,1024]{2,1,0:T(8,128)(2,1)S(1)}, u32[]{:S(2)}, u32[]{:S(2)}) async-start(bf16[32,8,1024]{2,1,0:T(8,128)(2,1)} %fusion.30), calls=%async_computation.2 | async-start | bytes 1048576 | tf_op jit(solution)/shard_map/all_to_all | solution.py:97
  76.2 0.0 reduce-scatter.2.cloned.1.call-start
  76.2 7.0 %all-gather.8.cloned.1.call-done = bf16[1,2048,1024]{2,1,0:T(8,128)(2,1)} async-done(((bf16[1,128,1024]{2,1,0:T(8,128)(2,1)}), bf16[1,2048,1024]{2,1,0:T(8,128)(2,1)}) %all-gather.8.cloned.1.call-update) | async-done | bytes 4194320 | tf_op jit(solution)/shard_map/all_gather | solution.py:102
  83.2 5.0 %fusion.6 = f32[256,2048]{1,0:T(8,128)} fusion(bf16[1,2048,1024]{2,1,0:T(8,128)(2,1)} %all-gather.8.cloned.1.call-done, bf16[32,8,1024]{2,1,0:T(8,128)(2,1)} %all-to-all-done), kind=kOutput, calls=%fused_computation.7 | convolution fusion | flops 1073741824 | bytes 6815744 | tf_op jit(solution)/shard_map/dot_general | solution.py:107
  88.2 21.5 %all-to-all-done.2 = bf16[32,8,1024]{2,1,0:T(8,128)(2,1)S(1)} async-done(((bf16[32,8,1024]{2,1,0:T(8,128)(2,1)}), bf16[32,8,1024]{2,1,0:T(8,128)(2,1)S(1)}, u32[]{:S(2)}, u32[]{:S(2)}) %all-to-all-start.2) | async-done | bytes 524320 | tf_op jit(solution)/shard_map/all_to_all | solution.py:97
  109.7 5.0 %convolution_convert_fusion = bf16[2048,1024]{1,0:T(8,128)(2,1)} fusion(bf16[32,8,1024]{2,1,0:T(8,128)(2,1)S(1)} %all-to-all-done.2, f32[256,2048]{1,0:T(8,128)} %fusion.6), kind=kOutput, calls=%fused_computation.9 | convolution fusion | flops 1078460416 | bytes 6815744 | tf_op jit(solution)/shard_map/dot_general | solution.py:123
  114.7 0.0 reduce-scatter.2.cloned.1.call-update
  114.7 0.0 all-gather.6.cloned.1.call-start
  114.7 0.5 all-gather.6.cloned.1.call-update
  115.3 37.6 %all-gather.10.cloned.1.call-done = bf16[1,2048,1024]{2,1,0:T(8,128)(2,1)} async-done(((bf16[1,128,1024]{2,1,0:T(8,128)(2,1)}), bf16[1,2048,1024]{2,1,0:T(8,128)(2,1)}) %all-gather.10.cloned.1.call-update) | async-done | bytes 4194320 | tf_op jit(solution)/shard_map/all_gather | solution.py:103
  152.9 4.9 %fusion.24 = bf16[32,8,1024]{2,1,0:T(8,128)(2,1)} fusion(bf16[1,2048,1024]{2,1,0:T(8,128)(2,1)} %all-gather.10.cloned.1.call-done, f32[256,2048]{1,0:T(8,128)} %fusion.6), kind=kOutput, calls=%fused_computation.83 | convolution fusion | flops 1076625408 | bytes 6815744 | tf_op jit(solution)/shard_map/dot_general | solution.py:109
  157.8 13.0 %all-to-all-start.1 = ((bf16[32,8,1024]{2,1,0:T(8,128)(2,1)}), bf16[32,8,1024]{2,1,0:T(8,128)(2,1)S(1)}, u32[]{:S(2)}, u32[]{:S(2)}) async-start(bf16[32,8,1024]{2,1,0:T(8,128)(2,1)} %fusion.24), calls=%async_computation.1 | async-start | bytes 1048576 | tf_op jit(solution)/shard_map/all_to_all | solution.py:116
  170.8 4.5 %fusion.11 = bf16[256,2048]{1,0:T(8,128)(2,1)S(1)} fusion(bf16[1,2048,1024]{2,1,0:T(8,128)(2,1)} %all-gather.10.cloned.1.call-done, f32[256,2048]{1,0:T(8,128)} %fusion.6, bf16[32,8,1024]{2,1,0:T(8,128)(2,1)S(1)} %all-to-all-done.2), kind=kOutput, calls=%fused_computation.12 | convolution fusion | flops 1078460416 | bytes 7864320 | tf_op jit(solution)/shard_map/dot_general | solution.py:110
  175.4 2.0 fusion.27
  177.4 26.9 %all-to-all-done.1 = bf16[32,8,1024]{2,1,0:T(8,128)(2,1)S(1)} async-done(((bf16[32,8,1024]{2,1,0:T(8,128)(2,1)}), bf16[32,8,1024]{2,1,0:T(8,128)(2,1)S(1)}, u32[]{:S(2)}, u32[]{:S(2)}) %all-to-all-start.1) | async-done | bytes 524320 | tf_op jit(solution)/shard_map/all_to_all | solution.py:116
  204.3 0.8 copy-done.3
  205.1 4.2 %all-to-all-start.3 = ((bf16[32,8,1024]{2,1,0:T(8,128)(2,1)}), bf16[32,8,1024]{2,1,0:T(8,128)(2,1)S(1)}, u32[]{:S(2)}, u32[]{:S(2)}) async-start(bf16[32,8,1024]{2,1,0:T(8,128)(2,1)} %fusion.27), calls=%async_computation.3 | async-start | bytes 1048576 | tf_op jit(solution)/shard_map/all_to_all | solution.py:117
  209.4 0.1 iota_compare_fusion.3
  209.5 0.1 eq.38
  209.6 1.4 copy.32
  210.9 1.8 fusion.16
  212.7 30.2 %all-to-all-done.3 = bf16[32,8,1024]{2,1,0:T(8,128)(2,1)S(1)} async-done(((bf16[32,8,1024]{2,1,0:T(8,128)(2,1)}), bf16[32,8,1024]{2,1,0:T(8,128)(2,1)S(1)}, u32[]{:S(2)}, u32[]{:S(2)}) %all-to-all-start.3) | async-done | bytes 524320 | tf_op jit(solution)/shard_map/all_to_all | solution.py:117
  242.9 5.0 %all-to-all-start.4 = ((bf16[256,16,128]{0,2,1:T(8,128)(2,1)}), bf16[256,16,128]{0,2,1:T(8,128)(2,1)S(1)}, u32[]{:S(2)}, u32[]{:S(2)}) async-start(bf16[256,16,128]{0,2,1:T(8,128)(2,1)} %bitcast.43), calls=%async_computation.4 | async-start | bytes 2097152 | tf_op jit(solution)/shard_map/all_to_all | solution.py:120
  247.9 0.3 fusion.186
  248.2 0.0 copy-done.2
  248.3 0.3 add_multiply_fusion
  248.6 3.6 %fusion.185 = (f32[128]{0:T(128)S(1)}, f32[128]{0:T(128)S(1)}, f32[128,1024]{1,0:T(8,128)S(1)}) fusion(f32[128]{0:T(128)S(1)} %add_rsqrt_fusion.1, f32[128]{0:T(128)S(1)} %broadcast_multiply_fusion.6, bf16[128,1024]{1,0:T(8,128)(2,1)S(1)} %copy-done, f32[128]{0:T(128)S(1)} %compare_convert_fusion, f32[1024]{0:T(1024)S(1)} %bitcast.117, ...), kind=kLoop, calls=%fused_computation.267 | loop fusion | flops 8912640 | bytes 1440256 | tf_op jit(solution)/shard_map/reduce_sum | solution.py:16
  252.2 0.0 copy-done.5
  252.2 1.1 fusion.42
  253.3 1.8 bitcast_convert_fusion
  255.1 8.6 %all-to-all-done.4 = bf16[256,16,128]{0,2,1:T(8,128)(2,1)S(1)} async-done(((bf16[256,16,128]{0,2,1:T(8,128)(2,1)}), bf16[256,16,128]{0,2,1:T(8,128)(2,1)S(1)}, u32[]{:S(2)}, u32[]{:S(2)}) %all-to-all-start.4) | async-done | bytes 1048608 | tf_op jit(solution)/shard_map/all_to_all | solution.py:120
  263.7 82.2 %all-gather.6.cloned.1.call-done = bf16[4096,1024]{1,0:T(8,128)(2,1)} async-done(((bf16[256,1024]{1,0:T(8,128)(2,1)}), bf16[4096,1024]{1,0:T(8,128)(2,1)}) %all-gather.6.cloned.1.call-update) | async-done | bytes 8388624 | tf_op jit(solution)/shard_map/all_gather | solution.py:104
  345.9 4.6 %convolution_convert_fusion.1 = bf16[16,128,1024]{2,1,0:T(8,128)(2,1)S(1)} fusion(bf16[16,256,1024]{2,1,0:T(8,128)(2,1)} %bitcast.94, bf16[256,16,128]{0,2,1:T(8,128)(2,1)S(1)} %all-to-all-done.4), kind=kOutput, calls=%fused_computation.11 | convolution fusion | flops 1075838976 | bytes 13631488 | tf_op jit(solution)/shard_map/rcw,rcd->rwd/dot_general | solution.py:51
  350.6 1.7 convert_reduce_fusion
  (21 shorter events, 0.1 us)
Async XLA Ops:
  7.2 10.0 %copy-start = (bf16[128,1024]{1,0:T(8,128)(2,1)S(1)}, bf16[128,1024]{1,0:T(8,128)(2,1)}, u32[]{:S(2)}) copy-start(bf16[128,1024]{1,0:T(8,128)(2,1)} %param.8) | copy-start | bytes 786436
  7.2 76.0 %all-gather.8.cloned.1.call-start = ((), (), s32[]{:S(2)}) async-start(), calls=%async_computation.8 | async-start | bytes 4456448 | tf_op jit(solution)/shard_map/all_gather | solution.py:102
  7.9 145.0 %all-gather.10.cloned.1.call-start = ((), (), s32[]{:S(2)}) async-start(), calls=%async_computation.9 | async-start | bytes 4456448 | tf_op jit(solution)/shard_map/all_gather | solution.py:103
  17.2 21.4 %copy-start.1 = (bf16[128,1024]{1,0:T(8,128)(2,1)S(1)}, bf16[128,1024]{1,0:T(8,128)(2,1)}, u32[]{:S(2)}) copy-start(bf16[128,1024]{1,0:T(8,128)(2,1)} %param.15) | copy-start | bytes 786436
  21.6 18.0 %copy-start.6 = (f32[128,2]{0,1:T(2,128)S(1)}, f32[128,2]{0,1:T(2,128)}, u32[]{:S(2)}) copy-start(f32[128,2]{0,1:T(2,128)} %param.11) | copy-start | bytes 3076
  21.6 50.5 %all-to-all-start = ((bf16[32,8,1024]{2,1,0:T(8,128)(2,1)}), bf16[32,8,1024]{2,1,0:T(8,128)(2,1)}, u32[]{:S(2)}, u32[]{:S(2)}) async-start(bf16[32,8,1024]{2,1,0:T(8,128)(2,1)} %fusion.23), calls=%async_computation | async-start | bytes 1048576 | tf_op jit(solution)/shard_map/all_to_all | solution.py:96
  72.1 37.6 %all-to-all-start.2 = ((bf16[32,8,1024]{2,1,0:T(8,128)(2,1)}), bf16[32,8,1024]{2,1,0:T(8,128)(2,1)S(1)}, u32[]{:S(2)}, u32[]{:S(2)}) async-start(bf16[32,8,1024]{2,1,0:T(8,128)(2,1)} %fusion.30), calls=%async_computation.2 | async-start | bytes 1048576 | tf_op jit(solution)/shard_map/all_to_all | solution.py:97
  76.2 177.2 %reduce-scatter.2.cloned.1.call-start = ((), (), s32[]{:S(2)}) async-start(), calls=%async_computation.7 | async-start | bytes 4456448 | tf_op jit(solution)/shard_map/reduce_scatter | solution.py:122
  114.7 231.2 %all-gather.6.cloned.1.call-start = ((), (), s32[]{:S(2)}) async-start(), calls=%async_computation.6 | async-start | bytes 8912896 | tf_op jit(solution)/shard_map/all_gather | solution.py:104
  157.8 46.5 %all-to-all-start.1 = ((bf16[32,8,1024]{2,1,0:T(8,128)(2,1)}), bf16[32,8,1024]{2,1,0:T(8,128)(2,1)S(1)}, u32[]{:S(2)}, u32[]{:S(2)}) async-start(bf16[32,8,1024]{2,1,0:T(8,128)(2,1)} %fusion.24), calls=%async_computation.1 | async-start | bytes 1048576 | tf_op jit(solution)/shard_map/all_to_all | solution.py:116
  170.8 4.5 %copy-start.7 = (bf16[1,2048,1024]{2,1,0:T(8,128)(2,1)S(1)}, bf16[1,2048,1024]{2,1,0:T(8,128)(2,1)}, u32[]{:S(2)}) copy-start(bf16[1,2048,1024]{2,1,0:T(8,128)(2,1)} %all-gather.8.cloned.1.call-done) | copy-start | bytes 12582916
  204.3 0.8 copy-start.3
  205.1 37.8 %all-to-all-start.3 = ((bf16[32,8,1024]{2,1,0:T(8,128)(2,1)}), bf16[32,8,1024]{2,1,0:T(8,128)(2,1)S(1)}, u32[]{:S(2)}, u32[]{:S(2)}) async-start(bf16[32,8,1024]{2,1,0:T(8,128)(2,1)} %fusion.27), calls=%async_computation.3 | async-start | bytes 1048576 | tf_op jit(solution)/shard_map/all_to_all | solution.py:117
  209.3 1.6 copy-start.4
  212.7 35.5 %copy-start.2 = (f32[128,1024]{1,0:T(8,128)S(1)}, f32[128,1024]{1,0:T(8,128)}, u32[]{:S(2)}) copy-start(f32[128,1024]{1,0:T(8,128)} %get-tuple-element.11) | copy-start | bytes 1572868
  242.9 20.8 %all-to-all-start.4 = ((bf16[256,16,128]{0,2,1:T(8,128)(2,1)}), bf16[256,16,128]{0,2,1:T(8,128)(2,1)S(1)}, u32[]{:S(2)}, u32[]{:S(2)}) async-start(bf16[256,16,128]{0,2,1:T(8,128)(2,1)} %bitcast.43), calls=%async_computation.4 | async-start | bytes 2097152 | tf_op jit(solution)/shard_map/all_to_all | solution.py:120
  248.2 4.0 %copy-start.5 = (f32[128,1024]{1,0:T(8,128)S(1)}, f32[128,1024]{1,0:T(8,128)}, u32[]{:S(2)}) copy-start(f32[128,1024]{1,0:T(8,128)} %fusion.16) | copy-start | bytes 1572868
Sparse Core Ops, SparseCore 0:
  11.0 72.1 all-gather.7
  86.2 66.6 all-gather.9
  157.1 91.2 reduce-scatter.1
  251.7 94.2 all-gather.5
where the time goes:
time: 360 us; the launch traced here: 359 us
  waiting for transfers between devices  246 us (68%)
  starting transfers between devices  43.3 us (12%)
  matrix products  30.8 us (9%)
  other arithmetic  16.6 us (5%)
  between operations  14.7 us (4%)
  local copies, waits for them, and re-layouts  7.63 us (2%)
    all_gather x1, waiting for transfers between devices, on_device(): lax.all_gather(recv_rows, 'rep', axis=0, tiled=True)  82.2 us
    all_gather x1, waiting for transfers between devices, on_device(): lax.all_gather(down_local, 'rep', axis=0, tiled=True)  37.6 us
    all_to_all x1, waiting for transfers between devices, on_device(): lax.all_to_all(row_grad, 'ep', split_axis=0, concat_axis=0, tiled=True)  30.2 us
    all_to_all x1, waiting for transfers between devices, on_device(): lax.all_to_all(send_rows, 'ep', split_axis=0, concat_axis=0, tiled=True)  29.9 us
    all_to_all x1, waiting for transfers between devices, on_device(): lax.all_to_all(expert_out, 'ep', split_axis=0, concat_axis=0, tiled=True)  26.9 us
    all_to_all x1, waiting for transfers between devices, on_device(): lax.all_to_all(send_slopes, 'ep', split_axis=0, concat_axis=0, tiled=True)  21.5 us
    all_to_all x1, starting transfers between devices, on_device(): lax.all_to_all(send_rows, 'ep', split_axis=0, concat_axis=0, tiled=True)  16.9 us
    all_to_all x1, starting transfers between devices, on_device(): lax.all_to_all(expert_out, 'ep', split_axis=0, concat_axis=0, tiled=True)  13 us
  transfers between devices with their start and end apart: 9, of which 8 were waited for; matrix products, arithmetic and copies ran while one was open for 13% of the time, Pallas kernels for 0%

commit v1 on v0

v1 whole, which is shorter than its diff:
```python
import functools

import jax
import jax.numpy as jnp
from jax import lax
from jax.experimental import pallas as pl
from jax.experimental.pallas import tpu as pltpu
from jax.sharding import PartitionSpec as P

MESH = pl.DeviceIdType.MESH
DMA = pltpu.SemaphoreType.DMA
F32 = jnp.float32
BF16 = jnp.bfloat16

EPS = 1e-05
SIDE = 4
CAP = 8
TAPS = 31
EDGE = 16
NEAR = ((0, 1), (1, -1))
ORDER = (0, -1, 1, 2)
LEAVE = (2, 1, -1, 0)


def wrap(i, n):
    return lax.rem(i + n, n)


def lane_iota(shape):
    return lax.broadcasted_iota(jnp.int32, shape, 1)


def landed(ref, sem):
    pltpu.make_async_copy(ref, ref, sem).wait()


def route_places(routes_ref, place_ref):
    count = routes_ref.shape[0]
    width = place_ref.shape[2]
    lane = lane_iota((count, 128))
    first, second = routes_ref[:, 0:1], routes_ref[:, 1:2]
    hot = [lane == first, lane == second]
    both = (hot[0].astype(F32) + hot[1].astype(F32)).astype(BF16)
    square = (count, count)
    earlier = lane_iota(square) < lax.broadcasted_iota(jnp.int32, square, 0)
    before = jnp.dot(earlier.astype(F32).astype(BF16), both, preferred_element_type=F32)
    wide = lane_iota((count, width)).astype(F32)
    for k, expert in enumerate((first, second)):
        rank = jnp.sum(jnp.where(hot[k], before, 0.0), axis=1, keepdims=True)
        row = expert.astype(F32) * (2 * CAP) + rank
        place_ref[2 * k] = (wide == row).astype(F32).astype(BF16)
        place_ref[2 * k + 1] = (wide == row + CAP).astype(F32).astype(BF16)


def contract_first(left, right):
    return lax.dot_general(left, right, (((0,), (0,)), ((), ())), preferred_element_type=F32)


def contract_last(left, right):
    return lax.dot_general(left, right, (((1,), (1,)), ((), ())), preferred_element_type=F32)


def pack_slopes(cot_ref, gate_ref, place_ref, out_ref):
    count, width = cot_ref.shape
    half = width // 2
    cot = cot_ref[...].astype(F32)
    parts = []
    for k in range(2):
        scaled = (gate_ref[:, k : k + 1] * cot).astype(BF16)
        parts += [scaled[:, :half], scaled[:, half:]]
    stacked = jnp.concatenate(parts, axis=0)
    place = place_ref[...].reshape(4 * count, -1)
    out_ref[...] = contract_first(place, stacked).astype(BF16).reshape(out_ref.shape)


def pack_rows(normed_ref, place_ref, out_ref):
    count, width = normed_ref.shape
    half = width // 2
    stacked = jnp.concatenate([normed_ref[:, :half], normed_ref[:, half:]], axis=0)
    low = place_ref[0] + place_ref[2]
    high = place_ref[1] + place_ref[3]
    place = jnp.concatenate([low, high], axis=0)
    out_ref[...] = contract_first(place, stacked).astype(BF16).reshape(out_ref.shape)


def over_rows(count, step, body):
    def run(i, carry):
        body(pl.ds(pl.multiple_of(i * step, step), step), pl.multiple_of(i * step, step))
        return carry

    lax.fori_loop(0, count // step, run, 0)


def normalize(values):
    center = values - jnp.mean(values, axis=-1, keepdims=True)
    inverse = lax.rsqrt(jnp.mean(center * center, axis=-1, keepdims=True) + EPS)
    return center * inverse, inverse


def norm_back(normed, inverse, upstream):
    mean_grad = jnp.mean(upstream, axis=-1, keepdims=True)
    mean_cross = jnp.mean(upstream * normed, axis=-1, keepdims=True)
    return inverse * (upstream - mean_grad - normed * mean_cross)


def silu_slope(values):
    part = jax.nn.sigmoid(values)
    return part + values * part * (1.0 - part)


def depthwise(pad_ref, kernel_ref, out_ref, reverse):
    count, width = out_ref.shape
    columns = 128

    def run(i, carry):
        at = pl.ds(pl.multiple_of(i * columns, columns), columns)
        total = jnp.zeros((count, columns), F32)
        for shift in range(8):
            part = None
            for base in range(0, 32, 8):
                j = base + shift - 1
                if j < 0 or j >= TAPS:
                    continue
                row = TAPS - 1 - j if reverse else j
                term = kernel_ref[row : row + 1, at] * pad_ref[base : base + count + 8, at]
                part = term if part is None else part + term
            if shift:
                part = pltpu.roll(part, count + 8 - shift, 0)
            total = total + part[:count]
        out_ref[:, at] = total
        return carry

    lax.fori_loop(0, width // columns, run, 0)


def front_norm(frames_ref, mask_ref, hat_ref, inv_ref, pad_ref):
    count, width = frames_ref.shape
    pad_ref[:EDGE] = jnp.zeros((EDGE, width), F32)
    pad_ref[EDGE + count :] = jnp.zeros((EDGE, width), F32)

    def body(at, start):
        hat, inverse = normalize(frames_ref[at].astype(F32))
        hat_ref[at] = hat
        inv_ref[at] = inverse
        pad_ref[pl.ds(start + EDGE, 16)] = hat * mask_ref[at]

    over_rows(count, 16, body)


def front_residual(frames_ref, conv_ref, res_ref, hat_ref, inv_ref, normed_ref):
    def body(at, start):
        residual = frames_ref[at].astype(F32) + jax.nn.silu(conv_ref[at])
        hat, inverse = normalize(residual)
        res_ref[at] = residual
        hat_ref[at] = hat
        inv_ref[at] = inverse
        normed_ref[at] = hat.astype(BF16)

    over_rows(frames_ref.shape[0], 16, body)


def back_mix(back_ref, place_ref, gate_ref, res_ref, out_ref):
    half = back_ref.shape[2]
    rows = back_ref[...].reshape(-1, half)
    for h in range(2):
        at = slice(h * half, (h + 1) * half)
        mixed = gate_ref[:, 0:1] * jnp.dot(place_ref[h], rows, preferred_element_type=F32)
        mixed += gate_ref[:, 1:2] * jnp.dot(place_ref[2 + h], rows, preferred_element_type=F32)
        out_ref[:, at] = (res_ref[:, at] + mixed).astype(BF16)


def back_slopes(back_ref, place_ref, grad_ref):
    half = back_ref.shape[2]
    rows = back_ref[...].reshape(-1, half)
    for h in range(2):
        pick = place_ref[h] + place_ref[2 + h]
        grad_ref[:, h * half : (h + 1) * half] = jnp.dot(pick, rows, preferred_element_type=F32)


def back_residual(cot_ref, hat_ref, inv_ref, conv_ref, grad_ref, pad_ref):
    def body(at, start):
        grad = cot_ref[at].astype(F32) + norm_back(hat_ref[at], inv_ref[at], grad_ref[at])
        grad_ref[at] = grad
        pad_ref[pl.ds(start + EDGE, 16)] = grad * silu_slope(conv_ref[at])

    over_rows(cot_ref.shape[0], 16, body)


def back_frames(first_ref, mask_ref, hat_ref, inv_ref, grad_ref, out_ref):
    def body(at, start):
        first = first_ref[at] * mask_ref[at]
        out_ref[at] = (grad_ref[at] + norm_back(hat_ref[at], inv_ref[at], first)).astype(BF16)

    over_rows(out_ref.shape[0], 16, body)


class Ring:
    def __init__(self, x_first):
        rep = lax.axis_index("rep")
        x, y = lax.rem(rep, SIDE), lax.div(rep, SIDE)
        self.x_first = x_first
        self.ep = lax.axis_index("ep")
        self.first, self.second = (x, y) if x_first else (y, x)
        self.started = []

    def index(self, first, second):
        first, second = wrap(first, SIDE), wrap(second, SIDE)
        return second * SIDE + first if self.x_first else first * SIDE + second

    def here(self):
        return self.index(self.first, self.second)

    def send(self, src, dst, send_sem, recv_sem, target):
        copy = pltpu.make_async_remote_copy(
            src_ref=src,
            dst_ref=dst,
            send_sem=send_sem,
            recv_sem=recv_sem,
            device_id=(self.ep, target),
            device_id_type=MESH,
        )
        copy.start()
        self.started.append(copy)

    def finish(self):
        for copy in self.started:
            copy.wait_send()


class Gather(Ring):
    def __init__(self, x_first, full, send_sem, near_sem, far_sem, row_sem, row_far_sem):
        super().__init__(x_first)
        self.full, self.send_sem = full, send_sem
        self.near_sem, self.far_sem = near_sem, far_sem
        self.row_sem, self.row_far_sem = row_sem, row_far_sem
        self.half = full.shape[1] // 2

    def piece(self, block, half):
        if half is None:
            return self.full.at[block]
        return self.full.at[block, pl.ds(half * self.half, self.half)]

    def push(self, block, half, target, sem):
        ref = self.piece(block, half)
        self.send(ref, ref, self.send_sem.at[len(self.started)], sem, target)

    def start(self):
        block = self.here()
        for d, s in NEAR:
            self.push(block, None, self.index(self.first + s, self.second), self.near_sem.at[d])
        self.across(0)

    def across(self, k):
        block = self.index(self.first + ORDER[k], self.second)
        for d, s in NEAR:
            self.push(block, None, self.index(self.first, self.second + s), self.row_sem.at[d, k])

    def relay_near(self):
        for d, s in NEAR:
            block = self.index(self.first - s, self.second)
            landed(self.piece(block, None), self.near_sem.at[d])
            self.push(block, d, self.index(self.first + s, self.second), self.far_sem.at[d])
            self.across(1 + d)

    def relay_far(self):
        block = self.index(self.first + 2, self.second)
        for d in (0, 1):
            landed(self.piece(block, d), self.far_sem.at[d])
        self.across(3)

    def relay_row(self, k):
        for d, s in NEAR:
            block = self.index(self.first + ORDER[k], self.second - s)
            landed(self.piece(block, None), self.row_sem.at[d, k])
            target = self.index(self.first, self.second + s)
            self.push(block, d, target, self.row_far_sem.at[d, k])

    def end_row(self, k):
        block = self.index(self.first + ORDER[k], self.second + 2)
        for d in (0, 1):
            landed(self.piece(block, d), self.row_far_sem.at[d, k])


class Scatter(Ring):
    def __init__(self, x_first, parts, via, near, part, via_last, near_last, *sems):
        super().__init__(x_first)
        self.parts, self.via, self.near, self.part = parts, via, near, part
        self.via_last, self.near_last = via_last, near_last
        self.sems = sems
        self.half = parts.shape[1] // 2

    def rows(self, half):
        return pl.ds(half * self.half, self.half)

    def block(self, step, i):
        return self.index(self.first + step, self.second + LEAVE[i])

    def send_far(self, i):
        send_sem, recv_sem = self.sems[0], self.sems[1]
        block = self.block(2, i)
        for d, s in NEAR:
            self.send(
                self.parts.at[block, self.rows(1 - d)],
                self.via.at[d, i],
                send_sem.at[d, i],
                recv_sem.at[d, i],
                self.index(self.first + s, self.second),
            )

    def send_near(self, d, i):
        send_sem, recv_sem = self.sems[2], self.sems[3]
        s = NEAR[d][1]
        block = self.block(s, i)
        landed(self.via.at[d, i], self.sems[1].at[d, i])
        rows = self.rows(1 - d)
        mine = self.parts[block, rows].astype(F32)
        self.parts[block, rows] = (mine + self.via[d, i].astype(F32)).astype(BF16)
        self.send(
            self.parts.at[block],
            self.near.at[d, i],
            send_sem.at[d, i],
            recv_sem.at[d, i],
            self.index(self.first + s, self.second),
        )

    def total(self, i):
        for d in (0, 1):
            landed(self.near.at[d, i], self.sems[3].at[d, i])
        mine = self.parts[self.block(0, i)].astype(F32)
        return mine + self.near[0, i].astype(F32) + self.near[1, i].astype(F32)

    def keep(self, i):
        self.part[i] = self.total(i).astype(BF16)

    def send_far_last(self):
        send_sem, recv_sem = self.sems[4], self.sems[5]
        for d, s in NEAR:
            self.send(
                self.part.at[0, self.rows(1 - d)],
                self.via_last.at[d],
                send_sem.at[d],
                recv_sem.at[d],
                self.index(self.first, self.second + s),
            )

    def send_near_last(self):
        send_sem, recv_sem = self.sems[6], self.sems[7]
        for d, s in NEAR:
            landed(self.via_last.at[d], self.sems[5].at[d])
            rows = self.rows(1 - d)
            mine = self.part[1 + d, rows].astype(F32)
            self.part[1 + d, rows] = (mine + self.via_last[d].astype(F32)).astype(BF16)
            self.send(
                self.part.at[1 + d],
                self.near_last.at[d],
                send_sem.at[d],
                recv_sem.at[d],
                self.index(self.first, self.second + s),
            )

    def last(self, out_ref):
        for d in (0, 1):
            landed(self.near_last.at[d], self.sems[7].at[d])
        mine = self.total(3)
        out_ref[...] = mine + self.near_last[0].astype(F32) + self.near_last[1].astype(F32)


class Exchange:
    def __init__(self, count, send, recv, send_sem, recv_sem):
        self.count = count
        self.send, self.recv = send, recv
        self.send_sem, self.recv_sem = send_sem, recv_sem
        self.ep, self.rep = lax.axis_index("ep"), lax.axis_index("rep")

    def copy(self, other, place):
        return pltpu.make_async_remote_copy(
            src_ref=self.send.at[other],
            dst_ref=self.recv.at[place],
            send_sem=self.send_sem.at[other],
            recv_sem=self.recv_sem.at[place],
            device_id=(other, self.rep),
            device_id_type=MESH,
        )

    def each(self, body):
        def run(i, carry):
            body(lax.rem(self.ep + i, self.count))
            return carry

        lax.fori_loop(1, self.count, run, 0)

    def start(self):
        self.each(lambda other: self.copy(other, self.ep).start())
        self.recv[self.ep] = self.send[self.ep]

    def arrive(self):
        self.each(lambda other: self.copy(other, other).wait_recv())

    def finish(self):
        self.each(lambda other: self.copy(other, other).wait_send())


def enter(count):
    ep, rep = lax.axis_index("ep"), lax.axis_index("rep")
    barrier = pltpu.get_barrier_semaphore()

    def run(i, carry):
        other = lax.rem(ep + i, count)
        pl.semaphore_signal(barrier, inc=1, device_id=(other, rep), device_id_type=MESH)
        return carry

    lax.fori_loop(1, count, run, 0)
    ring = Ring(True)
    for _, s in NEAR:
        for target in (ring.index(ring.first + s, ring.second), ring.index(ring.first, ring.second + s)):
            pl.semaphore_signal(barrier, inc=1, device_id=(ep, target), device_id_type=MESH)
    pl.semaphore_wait(barrier, count - 1 + 4)


def unpack(packed_ref, rows_ref):
    count, _, half = packed_ref.shape
    step = 4

    def run(i, carry):
        block = packed_ref[pl.ds(i * step, step)].astype(F32)
        at = pl.ds(pl.multiple_of(i * step * CAP, step * CAP), step * CAP)
        rows_ref[at, :half] = block[:, :CAP].reshape(step * CAP, half).astype(BF16)
        rows_ref[at, half:] = block[:, CAP:].reshape(step * CAP, half).astype(BF16)
        return carry

    lax.fori_loop(0, count // step, run, 0)


def pack(rows_ref, packed_ref):
    count, _, half = packed_ref.shape
    step = 4

    def run(i, carry):
        block = rows_ref[pl.ds(pl.multiple_of(i * step * CAP, step * CAP), step * CAP)]
        block = block.reshape(step, CAP, 2 * half)
        both = jnp.concatenate([block[:, :, :half], block[:, :, half:]], axis=1)
        packed_ref[pl.ds(i * step, step)] = both.astype(BF16)
        return carry

    lax.fori_loop(0, count // step, run, 0)


def weight_rows(weight_ref, j):
    pair = weight_ref[pl.ds(2 * j, 2)]
    return pair.reshape(2 * pair.shape[1], pair.shape[2])


def hidden_grads(slopes_in_ref, down_ref, wide_ref):
    def run(j, carry):
        wide_ref[j] = contract_last(slopes_in_ref[...], weight_rows(down_ref, j))
        return carry

    lax.fori_loop(0, wide_ref.shape[0], run, 0)


def hidden_units(rows_ref, up_ref, down_ref, wide_ref, hidden_ref, slopes_ref, out_ref, grad_ref):
    unit = hidden_ref.shape[2]
    out_ref[...] = jnp.zeros_like(out_ref)
    grad_ref[...] = jnp.zeros_like(grad_ref)

    def run(j, carry):
        pre = contract_last(rows_ref[...], weight_rows(up_ref, j))
        part = jax.nn.sigmoid(pre)
        hidden = (pre * part).astype(BF16)
        slopes = (wide_ref[j] * (part + pre * part * (1.0 - part))).astype(BF16)
        for i in range(2):
            hidden_ref[2 * j + i] = hidden[:, i * unit : (i + 1) * unit]
            slopes_ref[2 * j + i] = slopes[:, i * unit : (i + 1) * unit]
        out_ref[...] += jnp.dot(hidden, weight_rows(down_ref, j), preferred_element_type=F32)
        grad_ref[...] += jnp.dot(slopes, weight_rows(up_ref, j), preferred_element_type=F32)
        return carry

    lax.fori_loop(0, wide_ref.shape[0], run, 0)


def weight_grads(scatter, step, left_ref, right_ref):
    def run(i, carry):
        block = scatter.index(scatter.first + step, i)
        grads = contract_first(left_ref[block], right_ref[...])
        scatter.parts[block] = grads.astype(BF16)
        return carry

    lax.fori_loop(0, SIDE, run, 0)


def block_kernel(count, *refs):
    names = iter(refs)

    def take(n):
        return [next(names) for _ in range(n)]

    frames, mask, routes, gates, kernel, up_shard, down_shard, cot = take(8)
    block_out, frame_grad, up_grad, down_grad = take(4)
    up_all, down_all, local_sem = take(3)
    place, normed, hat1, inv1, pad, conv, res, hat2, inv2 = take(9)
    send_slopes, send_rows, recv_slopes, recv_rows = take(4)
    back_out, back_grad, recv_out, recv_grad = take(4)
    slopes_in, rows_in, wide, hidden, slopes, out_sum, grad_sum = take(7)
    normed_grad, first_grad = take(2)
    up_parts, down_parts = take(2)
    up_room, down_room = take(5), take(5)
    exchange_sems = [take(2) for _ in range(4)]
    gather_sems = [take(5) for _ in range(2)]
    scatter_sems = [take(8) for _ in range(2)]

    rep = lax.axis_index("rep")
    own = [
        pltpu.make_async_copy(up_shard, up_all.at[rep], local_sem.at[0]),
        pltpu.make_async_copy(down_shard, down_all.at[rep], local_sem.at[1]),
    ]
    for copy in own:
        copy.start()
    enter(count)
    for copy in own:
        copy.wait()
    gathers = [Gather(True, up_all, *gather_sems[0]), Gather(False, down_all, *gather_sems[1])]
    for gather in gathers:
        gather.start()

    to_slopes = Exchange(count, send_slopes, recv_slopes, *exchange_sems[0])
    to_rows = Exchange(count, send_rows, recv_rows, *exchange_sems[1])
    to_out = Exchange(count, back_out, recv_out, *exchange_sems[2])
    to_grad = Exchange(count, back_grad, recv_grad, *exchange_sems[3])

    route_places(routes, place)
    pack_slopes(cot, gates, place, send_slopes)
    to_slopes.start()
    front_norm(frames, mask, hat1, inv1, pad)
    depthwise(pad, kernel, conv, False)
    front_residual(frames, conv, res, hat2, inv2, normed)
    pack_rows(normed, place, send_rows)
    to_rows.start()

    for gather in gathers:
        gather.relay_near()
    for gather in gathers:
        gather.relay_row(0)
    for gather in gathers:
        gather.relay_far()
    for k in (1, 2, 3):
        for gather in gathers:
            gather.relay_row(k)
    to_slopes.arrive()
    unpack(recv_slopes, slopes_in)
    for k in range(SIDE):
        for gather in gathers:
            gather.end_row(k)
    hidden_grads(slopes_in, down_all, wide)
    to_rows.arrive()
    unpack(recv_rows, rows_in)
    hidden_units(rows_in, up_all, down_all, wide, hidden, slopes, out_sum, grad_sum)
    pack(out_sum, back_out)
    to_out.start()
    pack(grad_sum, back_grad)
    to_grad.start()

    scatters = [
        Scatter(False, up_parts, *up_room, *scatter_sems[0]),
        Scatter(True, down_parts, *down_room, *scatter_sems[1]),
    ]
    sides = [(slopes, rows_in), (hidden, slopes_in)]
    for scatter, (left, right) in zip(scatters, sides):
        weight_grads(scatter, 2, left, right)
        for i in range(SIDE):
            scatter.send_far(i)
    for step in (1, -1, 0):
        for scatter, (left, right) in zip(scatters, sides):
            weight_grads(scatter, step, left, right)
    for i in range(SIDE):
        for scatter in scatters:
            for d in (0, 1):
                scatter.send_near(d, i)
    for i in range(3):
        for scatter in scatters:
            scatter.keep(i)
            if i == 0:
                scatter.send_far_last()
    for scatter in scatters:
        scatter.send_near_last()

    to_out.arrive()
    back_mix(recv_out, place, gates, res, block_out)
    to_grad.arrive()
    back_slopes(recv_grad, place, normed_grad)
    back_residual(cot, hat2, inv2, conv, normed_grad, pad)
    depthwise(pad, kernel, first_grad, True)
    back_frames(first_grad, mask, hat1, inv1, normed_grad, frame_grad)
    for scatter, out in zip(scatters, (up_grad, down_grad)):
        scatter.last(out)

    for exchange in (to_slopes, to_rows, to_out, to_grad):
        exchange.finish()
    for ring in gathers + scatters:
        ring.finish()


def on_device(frames, lengths, routes, gate_weights, kernel, up_weight, down_weight, cotangent):
    experts = lax.axis_size("ep")
    reps = lax.axis_size("rep")
    count, width = frames.shape
    unit = up_weight.shape[1]
    rows = experts * CAP
    half = width // 2
    positions = lax.broadcasted_iota(jnp.int32, (count, 1), 0)
    mask = (positions < lengths[0]).astype(F32)
    gates = gate_weights * mask

    vmem = pltpu.VMEM
    packed = vmem((experts, 2 * CAP, half), BF16)
    grid32 = vmem((count, width), F32)
    column = vmem((count, 1), F32)
    weights = vmem((reps, unit, width), BF16)
    room = [
        vmem((2, SIDE, unit // 2, width), BF16),
        vmem((2, SIDE, unit, width), BF16),
        vmem((3, unit, width), BF16),
        vmem((2, unit // 2, width), BF16),
        vmem((2, unit, width), BF16),
    ]
    scratch = [weights, weights, DMA((2,))]
    scratch += [vmem((4, count, 2 * rows), BF16), vmem((count, width), BF16)]
    scratch += [grid32, column, vmem((count + 2 * EDGE, width), F32), grid32, grid32, grid32, column]
    scratch += [packed] * 8
    scratch += [vmem((rows, width), BF16)] * 2
    scratch += [vmem((reps // 2, rows, 2 * unit), F32)]
    scratch += [vmem((reps, rows, unit), BF16)] * 2
    scratch += [vmem((rows, width), F32)] * 2
    scratch += [grid32, grid32, weights, weights] + room + room
    scratch += [DMA((experts,))] * 8
    scratch += [DMA((20,)), DMA((2,)), DMA((2,)), DMA((2, SIDE)), DMA((2, SIDE))] * 2
    scratch += ([DMA((2, SIDE))] * 4 + [DMA((2,))] * 4) * 2

    in_vmem = pl.BlockSpec(memory_space=pltpu.VMEM)
    anywhere = pl.BlockSpec(memory_space=pl.ANY)
    block_out, frame_grad, up_grad, down_grad = pl.pallas_call(
        functools.partial(block_kernel, experts),
        out_shape=[jax.ShapeDtypeStruct((count, width), BF16)] * 2
        + [jax.ShapeDtypeStruct((unit, width), F32)] * 2,
        in_specs=[in_vmem] * 5 + [anywhere] * 2 + [in_vmem],
        out_specs=[in_vmem] * 4,
        scratch_shapes=scratch,
        compiler_params=pltpu.CompilerParams(
            collective_id=0, has_side_effects=True, vmem_limit_bytes=58 << 20
        ),
        cost_estimate=pl.CostEstimate(
            flops=12 * rows * reps * unit * width, bytes_accessed=8 << 20, transcendentals=0
        ),
    )(frames, mask, routes, gates, kernel, up_weight[0], down_weight[0], cotangent)
    return block_out, frame_grad, up_grad[None], down_grad[None]


def solution(mesh):
    in_specs = (
        P(("ep", "rep"), None),
        P(("ep", "rep")),
        P(("ep", "rep"), None),
        P(("ep", "rep"), None),
        P(),
        P("ep", "rep", None),
        P("ep", "rep", None),
        P(("ep", "rep"), None),
    )
    out_specs = (
        P(("ep", "rep"), None),
        P(("ep", "rep"), None),
        P("ep", "rep", None),
        P("ep", "rep", None),
    )
    return jax.shard_map(
        on_device, mesh=mesh, in_specs=in_specs, out_specs=out_specs, check_vma=False
    )
```

time: 360 us -> 141 us (0.39)
  waiting for transfers between devices: 246 us -> 0 us
  Pallas kernels: 0 us -> 132 us
  starting transfers between devices: 43.3 us -> 0 us
  matrix products: 30.8 us -> 0 us
  other arithmetic: 16.6 us -> 1.36 us
  between operations: 14.7 us -> 1.32 us
    pallas_call x0 -> x1, Pallas kernels: none -> 132 us  [on_device(): pl.pallas_call(functools.partial(block_kernel, experts), out_shape=[jax.S...]
    all_gather x3 -> x0, waiting for transfers between devices: 127 us -> none  [the longest x1 82.2 us: on_device(): lax.all_gather(recv_rows, 'rep', axis=0, tiled=True)]
    all_to_all x5 -> x0, waiting for transfers between devices: 117 us -> none  [the longest x1 30.2 us: on_device(): lax.all_to_all(row_grad, 'ep', split_axis=0, concat_axis=0, tiled=True)]
    all_to_all x5 -> x0, starting transfers between devices: 43.2 us -> none  [the longest x1 16.9 us: on_device(): lax.all_to_all(send_rows, 'ep', split_axis=0, concat_axis=0, tiled=True)]
    dot_general x11 -> x0, matrix products: 30.8 us -> none  [the longest x1 4.97 us: on_device(): lax.dot_general(recv_rows, up_all, contract, preferred_element_type=jnp.f...]
    reduce_sum x7 -> x0, other arithmetic: 10.8 us -> none  [the longest x2 4.1 us: normalize(): center = values - jnp.mean(values, axis=-1, keepdims=True)]
    unnamed x17 -> x16, local copies, waits for them, and re-layouts: 1.6 us -> 5.99 us
  transfers between devices with their start and end apart: 9 -> 0, of which waited for: 8 -> 0; matrix products, arithmetic and copies ran while one was open for 13% -> 0% of each run, Pallas kernels for 0% -> 0%
where the time goes in v1:
time: 141 us
  Pallas kernels  132 us (94%)
  local copies, waits for them, and re-layouts  5.99 us (4%)
    pallas_call x1, Pallas kernels, on_device(): pl.pallas_call(functools.partial(block_kernel, experts), out_shape=[jax.S...  132 us
    unnamed x16, local copies, waits for them, and re-layouts  5.99 us

profile of v1, /device:TPU:1, one launch (start us, length us, event | category | flops | bytes accessed | tf_op | source)
XLA Modules:
  0.0 140.9 jit_solution(4075712524236269099)
XLA Ops:
  1.3 0.0 copy-start.3
  1.3 0.7 copy-done.3
  2.0 0.0 copy-start.4
  2.0 0.7 copy.16.refs_2_
  2.7 0.0 copy-done.4
  2.7 0.1 copy.14
  2.8 0.7 broadcast_multiply_fusion.refs_3_
  3.5 0.6 fusion.refs_1_
  4.2 132.3 %shard_map.111 = (bf16[128,1024]{1,0:T(8,128)(2,1)}, bf16[128,1024]{1,0:T(8,128)(2,1)}, f32[128,1024]{1,0:T(8,128)}, f32[128,1024]{1,0:T(8,128)}) custom-call(bf16[128,1024]{1,0:T(8,128)(2,1)} %refs_0_.1, f32[128,1]{1,0:T(8,128)} %fusion.refs_1_, s32[128,2]{1,0:T(8,128)} %copy.16.refs_2_, f32[128,2]{1,0:T(8,128)} %broadcast_multiply_fusion.refs_3_, ...), custom_call_target="tpu_custom_call" | custom-call | flops 6442450944 | bytes 8388608 | tf_op jit(solution)/shard_map/pallas_call | solution.py:640
  136.5 0.0 copy-start.2
  136.5 0.0 copy-start.1
  136.5 1.7 %copy.22 = bf16[128,1024]{1,0:T(8,128)(2,1)} copy(bf16[128,1024]{1,0:T(8,128)(2,1)} %get-tuple-element.16) | data formatting | bytes 524288
  138.2 0.0 copy-done.2
  138.2 0.7 copy.23
  138.9 0.0 copy-done.1
  138.9 0.0 copy-start
  138.9 0.8 copy.24
  139.7 0.4 copy-done
  140.2 0.8 copy.25
  (1 shorter events, 0.0 us)
Async XLA Ops:
  1.3 0.7 copy-start.3
  2.0 0.7 copy-start.4
  136.5 1.8 %copy-start.2 = (bf16[128,1024]{1,0:T(8,128)(2,1)S(1)}, bf16[128,1024]{1,0:T(8,128)(2,1)}, u32[]{:S(2)}) copy-start(bf16[128,1024]{1,0:T(8,128)(2,1)} %get-tuple-element.17) | copy-start | bytes 786436
  136.5 2.5 %copy-start.1 = (f32[128,1024]{1,0:T(8,128)S(1)}, f32[128,1024]{1,0:T(8,128)}, u32[]{:S(2)}) copy-start(f32[128,1024]{1,0:T(8,128)} %get-tuple-element.10) | copy-start | bytes 1572868
  138.9 1.2 copy-start

commit v2 on v1

v2 whole, which is shorter than its diff:
```python
import functools

import jax
import jax.numpy as jnp
from jax import lax
from jax.experimental import pallas as pl
from jax.experimental.pallas import tpu as pltpu
from jax.sharding import PartitionSpec as P

MESH = pl.DeviceIdType.MESH
DMA = pltpu.SemaphoreType.DMA
F32 = jnp.float32
BF16 = jnp.bfloat16

EPS = 1e-05
SIDE = 4
CAP = 8
TAPS = 31
EDGE = 16
NEAR = ((0, 1), (1, -1))
ORDER = (0, -1, 1, 2)
LEAVE = (2, 1, -1, 0)


def wrap(i, n):
    return lax.rem(i + n, n)


def lane_iota(shape):
    return lax.broadcasted_iota(jnp.int32, shape, 1)


def landed(ref, sem):
    pltpu.make_async_copy(ref, ref, sem).wait()


def to_column(row):
    count = row.shape[1]
    square = (count, count)
    here = lane_iota(square) == lax.broadcasted_iota(jnp.int32, square, 0)
    return jnp.sum(jnp.where(here, row, 0.0), axis=1, keepdims=True)


def route_places(routes_ref, rank_ref, place_ref):
    experts = place_ref.shape[0] // (2 * CAP)
    count = routes_ref.shape[1]
    shape = (experts, count)
    sub = lax.broadcasted_iota(jnp.int32, shape, 0)
    hot = [sub == routes_ref[k : k + 1] for k in range(2)]
    both = (hot[0].astype(F32) + hot[1].astype(F32)).astype(BF16)
    square = (count, count)
    earlier = lax.broadcasted_iota(jnp.int32, square, 0) < lane_iota(square)
    before = jnp.dot(both, earlier.astype(F32).astype(BF16), preferred_element_type=F32)
    tall = lax.broadcasted_iota(jnp.int32, (place_ref.shape[0], count), 0).astype(F32)
    for k in range(2):
        rank = jnp.sum(jnp.where(hot[k], before, 0.0), axis=0, keepdims=True)
        row = routes_ref[k : k + 1].astype(F32) * (2 * CAP) + rank
        rank_ref[k : k + 1] = row
        for h in range(2):
            at = slice((2 * k + h) * count, (2 * k + h + 1) * count)
            place_ref[:, at] = (tall == row + h * CAP).astype(F32).astype(BF16)


def turn_places(rank_ref, turned_ref):
    _, count, width = turned_ref.shape
    wide = lane_iota((count, width)).astype(F32)
    for k in range(2):
        row = to_column(rank_ref[k : k + 1])
        for h in range(2):
            turned_ref[2 * k + h] = (wide == row + h * CAP).astype(F32).astype(BF16)


def live_columns(length_ref, gates_ref, mask_ref, gate_ref):
    count = mask_ref.shape[0]
    positions = lax.broadcasted_iota(jnp.int32, (count, 1), 0)
    mask = (positions < length_ref[...]).astype(F32)
    mask_ref[...] = mask
    for k in range(2):
        gate_ref[k] = to_column(gates_ref[k : k + 1]) * mask


def contract_first(left, right):
    return lax.dot_general(left, right, (((0,), (0,)), ((), ())), preferred_element_type=F32)


def contract_last(left, right):
    return lax.dot_general(left, right, (((1,), (1,)), ((), ())), preferred_element_type=F32)


def pack_slopes(cot_ref, gate_ref, place_ref, out_ref):
    width = cot_ref.shape[1]
    half = width // 2
    cot = cot_ref[...].astype(F32)
    parts = []
    for k in range(2):
        scaled = (gate_ref[k] * cot).astype(BF16)
        parts += [scaled[:, :half], scaled[:, half:]]
    stacked = jnp.concatenate(parts, axis=0)
    packed = jnp.dot(place_ref[...], stacked, preferred_element_type=F32)
    out_ref[...] = packed.astype(BF16).reshape(out_ref.shape)


def pack_rows(normed_ref, place_ref, out_ref):
    width = normed_ref.shape[1]
    half = width // 2
    stacked = jnp.concatenate([normed_ref[:, :half], normed_ref[:, half:]], axis=0)
    middle = place_ref.shape[1] // 2
    place = place_ref[:, :middle] + place_ref[:, middle:]
    packed = jnp.dot(place, stacked, preferred_element_type=F32)
    out_ref[...] = packed.astype(BF16).reshape(out_ref.shape)


def over_rows(count, step, body):
    def run(i, carry):
        body(pl.ds(pl.multiple_of(i * step, step), step), pl.multiple_of(i * step, step))
        return carry

    lax.fori_loop(0, count // step, run, 0)


def normalize(values):
    center = values - jnp.mean(values, axis=-1, keepdims=True)
    inverse = lax.rsqrt(jnp.mean(center * center, axis=-1, keepdims=True) + EPS)
    return center * inverse, inverse


def norm_back(normed, inverse, upstream):
    mean_grad = jnp.mean(upstream, axis=-1, keepdims=True)
    mean_cross = jnp.mean(upstream * normed, axis=-1, keepdims=True)
    return inverse * (upstream - mean_grad - normed * mean_cross)


def silu_slope(values):
    part = jax.nn.sigmoid(values)
    return part + values * part * (1.0 - part)


def depthwise(pad_ref, kernel_ref, out_ref, reverse):
    count, width = out_ref.shape
    columns = 128

    def run(i, carry):
        at = pl.ds(pl.multiple_of(i * columns, columns), columns)
        total = jnp.zeros((count, columns), F32)
        for shift in range(8):
            part = None
            for base in range(0, 32, 8):
                j = base + shift - 1
                if j < 0 or j >= TAPS:
                    continue
                row = TAPS - 1 - j if reverse else j
                term = kernel_ref[row : row + 1, at] * pad_ref[base : base + count + 8, at]
                part = term if part is None else part + term
            if shift:
                part = pltpu.roll(part, count + 8 - shift, 0)
            total = total + part[:count]
        out_ref[:, at] = total
        return carry

    lax.fori_loop(0, width // columns, run, 0)


def front_norm(frames_ref, mask_ref, hat_ref, inv_ref, pad_ref):
    count, width = frames_ref.shape
    pad_ref[:EDGE] = jnp.zeros((EDGE, width), F32)
    pad_ref[EDGE + count :] = jnp.zeros((EDGE, width), F32)

    def body(at, start):
        hat, inverse = normalize(frames_ref[at].astype(F32))
        hat_ref[at] = hat
        inv_ref[at] = inverse
        pad_ref[pl.ds(start + EDGE, 16)] = hat * mask_ref[at]

    over_rows(count, 16, body)


def front_residual(frames_ref, conv_ref, res_ref, hat_ref, inv_ref, normed_ref):
    def body(at, start):
        residual = frames_ref[at].astype(F32) + jax.nn.silu(conv_ref[at])
        hat, inverse = normalize(residual)
        res_ref[at] = residual
        hat_ref[at] = hat
        inv_ref[at] = inverse
        normed_ref[at] = hat.astype(BF16)

    over_rows(frames_ref.shape[0], 16, body)


def back_mix(back_ref, place_ref, gate_ref, res_ref, out_ref):
    half = back_ref.shape[2]
    rows = back_ref[...].reshape(-1, half)
    for h in range(2):
        at = slice(h * half, (h + 1) * half)
        mixed = gate_ref[0] * jnp.dot(place_ref[h], rows, preferred_element_type=F32)
        mixed += gate_ref[1] * jnp.dot(place_ref[2 + h], rows, preferred_element_type=F32)
        out_ref[:, at] = (res_ref[:, at] + mixed).astype(BF16)


def back_slopes(back_ref, place_ref, grad_ref):
    half = back_ref.shape[2]
    rows = back_ref[...].reshape(-1, half)
    for h in range(2):
        pick = place_ref[h] + place_ref[2 + h]
        grad_ref[:, h * half : (h + 1) * half] = jnp.dot(pick, rows, preferred_element_type=F32)


def back_residual(cot_ref, hat_ref, inv_ref, conv_ref, grad_ref, pad_ref):
    def body(at, start):
        grad = cot_ref[at].astype(F32) + norm_back(hat_ref[at], inv_ref[at], grad_ref[at])
        grad_ref[at] = grad
        pad_ref[pl.ds(start + EDGE, 16)] = grad * silu_slope(conv_ref[at])

    over_rows(cot_ref.shape[0], 16, body)


def back_frames(first_ref, mask_ref, hat_ref, inv_ref, grad_ref, out_ref):
    def body(at, start):
        first = first_ref[at] * mask_ref[at]
        out_ref[at] = (grad_ref[at] + norm_back(hat_ref[at], inv_ref[at], first)).astype(BF16)

    over_rows(out_ref.shape[0], 16, body)


class Ring:
    def __init__(self, x_first):
        rep = lax.axis_index("rep")
        x, y = lax.rem(rep, SIDE), lax.div(rep, SIDE)
        self.x_first = x_first
        self.ep = lax.axis_index("ep")
        self.first, self.second = (x, y) if x_first else (y, x)

    def device(self, first, second):
        first, second = wrap(first, SIDE), wrap(second, SIDE)
        return second * SIDE + first if self.x_first else first * SIDE + second

    def here(self):
        return self.slot(self.first, self.second)

    def slot(self, first, second):
        return wrap(first, SIDE) * SIDE + wrap(second, SIDE)

    def send(self, src, dst, recv_sem, target):
        pltpu.make_async_remote_copy(
            src_ref=src,
            dst_ref=dst,
            send_sem=self.send_sem.at[0],
            recv_sem=recv_sem,
            device_id=(self.ep, target),
            device_id_type=MESH,
        ).start()

    def finish(self, blocks):
        landed(blocks.at[pl.ds(0, SIDE * SIDE - 1)], self.send_sem.at[0])


class Gather(Ring):
    def __init__(self, x_first, full, send_sem, near_sem, far_sem, row_sem, row_far_sem):
        super().__init__(x_first)
        self.full, self.send_sem = full, send_sem
        self.near_sem, self.far_sem = near_sem, far_sem
        self.row_sem, self.row_far_sem = row_sem, row_far_sem
        self.half = full.shape[1] // 2

    def piece(self, block, half):
        if half is None:
            return self.full.at[block]
        return self.full.at[block, pl.ds(half * self.half, self.half)]

    def push(self, block, half, target, sem):
        ref = self.piece(block, half)
        self.send(ref, ref, sem, target)

    def start(self):
        block = self.here()
        for d, s in NEAR:
            self.push(block, None, self.device(self.first + s, self.second), self.near_sem.at[d])
        self.across(0)

    def across(self, k):
        block = self.slot(self.first + ORDER[k], self.second)
        for d, s in NEAR:
            target = self.device(self.first, self.second + s)
            self.push(block, None, target, self.row_sem.at[d, k])

    def relay_near(self):
        for d, s in NEAR:
            block = self.slot(self.first - s, self.second)
            landed(self.piece(block, None), self.near_sem.at[d])
            self.push(block, d, self.device(self.first + s, self.second), self.far_sem.at[d])
            self.across(1 + d)

    def relay_far(self):
        block = self.slot(self.first + 2, self.second)
        for d in (0, 1):
            landed(self.piece(block, d), self.far_sem.at[d])
        self.across(3)

    def relay_row(self, k):
        for d, s in NEAR:
            block = self.slot(self.first + ORDER[k], self.second - s)
            landed(self.piece(block, None), self.row_sem.at[d, k])
            target = self.device(self.first, self.second + s)
            self.push(block, d, target, self.row_far_sem.at[d, k])

    def end_row(self, k):
        block = self.slot(self.first + ORDER[k], self.second + 2)
        for d in (0, 1):
            landed(self.piece(block, d), self.row_far_sem.at[d, k])


class Scatter(Ring):
    def __init__(self, x_first, parts, via, near, part, via_last, near_last, send_sem, *sems):
        super().__init__(x_first)
        self.parts, self.via, self.near, self.part = parts, via, near, part
        self.via_last, self.near_last = via_last, near_last
        self.send_sem = send_sem
        self.via_sem, self.near_sem, self.via_last_sem, self.near_last_sem = sems
        self.half = parts.shape[1] // 2

    def rows(self, half):
        return pl.ds(half * self.half, self.half)

    def block(self, step, i):
        return self.slot(self.first + step, self.second + LEAVE[i])

    def send_far(self, i):
        block = self.block(2, i)
        for d, s in NEAR:
            target = self.device(self.first + s, self.second)
            src = self.parts.at[block, self.rows(1 - d)]
            self.send(src, self.via.at[d, i], self.via_sem.at[d, i], target)

    def send_near(self, d, i):
        s = NEAR[d][1]
        block = self.block(s, i)
        landed(self.via.at[d, i], self.via_sem.at[d, i])
        rows = self.rows(1 - d)
        mine = self.parts[block, rows].astype(F32)
        self.parts[block, rows] = (mine + self.via[d, i].astype(F32)).astype(BF16)
        target = self.device(self.first + s, self.second)
        self.send(self.parts.at[block], self.near.at[d, i], self.near_sem.at[d, i], target)

    def total(self, i):
        for d in (0, 1):
            landed(self.near.at[d, i], self.near_sem.at[d, i])
        mine = self.parts[self.block(0, i)].astype(F32)
        return mine + self.near[0, i].astype(F32) + self.near[1, i].astype(F32)

    def keep(self, i):
        self.part[i] = self.total(i).astype(BF16)

    def send_far_last(self):
        for d, s in NEAR:
            target = self.device(self.first, self.second + s)
            src = self.part.at[0, self.rows(1 - d)]
            self.send(src, self.via_last.at[d], self.via_last_sem.at[d], target)

    def send_near_last(self, d):
        landed(self.via_last.at[d], self.via_last_sem.at[d])
        rows = self.rows(1 - d)
        mine = self.part[1 + d, rows].astype(F32)
        self.part[1 + d, rows] = (mine + self.via_last[d].astype(F32)).astype(BF16)
        target = self.device(self.first, self.second + NEAR[d][1])
        self.send(self.part.at[1 + d], self.near_last.at[d], self.near_last_sem.at[d], target)

    def last(self, out_ref):
        for d in (0, 1):
            landed(self.near_last.at[d], self.near_last_sem.at[d])
        mine = self.total(3)
        out_ref[...] = mine + self.near_last[0].astype(F32) + self.near_last[1].astype(F32)


class Exchange:
    def __init__(self, count, send, recv, send_sem, recv_sem):
        self.count = count
        self.send, self.recv = send, recv
        self.send_sem, self.recv_sem = send_sem, recv_sem
        self.ep, self.rep = lax.axis_index("ep"), lax.axis_index("rep")

    def copy(self, other, place):
        return pltpu.make_async_remote_copy(
            src_ref=self.send.at[other],
            dst_ref=self.recv.at[place],
            send_sem=self.send_sem.at[0],
            recv_sem=self.recv_sem.at[0],
            device_id=(other, self.rep),
            device_id_type=MESH,
        )

    def each(self, body):
        def run(i, carry):
            body(lax.rem(self.ep + i, self.count))
            return carry

        lax.fori_loop(1, self.count, run, 0)

    def start(self):
        self.each(lambda other: self.copy(other, self.ep).start())
        self.recv[self.ep] = self.send[self.ep]

    def arrive(self):
        landed(self.recv.at[pl.ds(0, self.count - 1)], self.recv_sem.at[0])

    def finish(self):
        landed(self.send.at[pl.ds(0, self.count - 1)], self.send_sem.at[0])


def announce(count):
    ep, rep = lax.axis_index("ep"), lax.axis_index("rep")
    barrier = pltpu.get_barrier_semaphore()

    def run(i, carry):
        other = lax.rem(ep + i, count)
        pl.semaphore_signal(barrier, inc=1, device_id=(other, rep), device_id_type=MESH)
        return carry

    lax.fori_loop(1, count, run, 0)
    ring = Ring(True)
    for _, s in NEAR:
        for target in (ring.device(ring.first + s, ring.second), ring.device(ring.first, ring.second + s)):
            pl.semaphore_signal(barrier, inc=1, device_id=(ep, target), device_id_type=MESH)


def enter(count):
    pl.semaphore_wait(pltpu.get_barrier_semaphore(), count - 1 + 4)


def unpack(packed_ref, rows_ref):
    count, _, half = packed_ref.shape
    step = 4

    def run(i, carry):
        block = packed_ref[pl.ds(i * step, step)].astype(F32)
        at = pl.ds(pl.multiple_of(i * step * CAP, step * CAP), step * CAP)
        rows_ref[at, :half] = block[:, :CAP].reshape(step * CAP, half).astype(BF16)
        rows_ref[at, half:] = block[:, CAP:].reshape(step * CAP, half).astype(BF16)
        return carry

    lax.fori_loop(0, count // step, run, 0)


def pack(rows_ref, packed_ref):
    count, _, half = packed_ref.shape
    step = 4

    def run(i, carry):
        block = rows_ref[pl.ds(pl.multiple_of(i * step * CAP, step * CAP), step * CAP)]
        block = block.reshape(step, CAP, 2 * half)
        both = jnp.concatenate([block[:, :, :half], block[:, :, half:]], axis=1)
        packed_ref[pl.ds(i * step, step)] = both.astype(BF16)
        return carry

    lax.fori_loop(0, count // step, run, 0)


def weight_rows(weight_ref, j):
    pair = weight_ref[pl.ds(2 * j, 2)]
    return pair.reshape(2 * pair.shape[1], pair.shape[2])


def hidden_grads(slopes_in_ref, down_ref, wide_ref):
    unit = down_ref.shape[1]

    def run(j, carry):
        grads = contract_last(slopes_in_ref[...], weight_rows(down_ref, j))
        wide_ref[2 * j] = grads[:, :unit]
        wide_ref[2 * j + 1] = grads[:, unit:]
        return carry

    lax.fori_loop(0, down_ref.shape[0] // 2, run, 0)


def hidden_units(rows_ref, up_ref, wide_ref, hidden_ref, slopes_ref):
    unit = up_ref.shape[1]

    def run(j, carry):
        both = contract_last(rows_ref[...], weight_rows(up_ref, j))
        for i in range(2):
            pre = both[:, i * unit : (i + 1) * unit]
            slot = 2 * j + i
            other = lax.rem(slot, SIDE) * SIDE + lax.div(slot, SIDE)
            part = 0.5 * jnp.tanh(0.5 * pre) + 0.5
            value = pre * part
            slopes = wide_ref[other] * (part + value * (1.0 - part))
            at = pl.ds(pl.multiple_of(other * unit, unit), unit)
            hidden_ref[:, at] = value.astype(BF16)
            at = pl.ds(pl.multiple_of(slot * unit, unit), unit)
            slopes_ref[:, at] = slopes.astype(BF16)
        return carry

    lax.fori_loop(0, up_ref.shape[0] // 2, run, 0)


def project(left_ref, weight_ref, sum_ref):
    tile = 256

    def run(j, carry):
        at = pl.ds(pl.multiple_of(j * tile, tile), tile)
        right = weight_ref[:, :, at].reshape(-1, tile)
        sum_ref[:, at] = jnp.dot(left_ref[...], right, preferred_element_type=F32)
        return carry

    lax.fori_loop(0, sum_ref.shape[1] // tile, run, 0)


def weight_grads(scatter, step, left_ref, right_ref):
    unit = scatter.parts.shape[1]
    first = scatter.slot(scatter.first + step, 0)

    def run(i, carry):
        block = first + 2 * i
        left = left_ref[:, pl.ds(pl.multiple_of(block * unit, 2 * unit), 2 * unit)]
        grads = contract_first(left, right_ref[...]).astype(BF16)
        scatter.parts[pl.ds(block, 2)] = grads.reshape(2, unit, -1)
        return carry

    lax.fori_loop(0, SIDE // 2, run, 0)


def block_kernel(count, *refs):
    names = iter(refs)

    def take(n):
        return [next(names) for _ in range(n)]

    length, routes, gates = take(3)
    inputs, outputs = take(5), take(4)
    up_all, down_all = take(2)
    frames, kernel, cot = take(3)
    block_out, frame_grad, up_grad, down_grad = take(4)
    ranks, place, turned, mask, gate = take(5)
    normed, hat1, inv1, pad, conv, res, hat2, inv2 = take(8)
    send_slopes, send_rows, recv_slopes, recv_rows = take(4)
    back_out, back_grad, recv_out, recv_grad = take(4)
    slopes_in, rows_in, wide, hidden, slopes, row_sum = take(6)
    normed_grad, first_grad = take(2)
    up_parts, down_parts = take(2)
    up_room, down_room = take(5), take(5)
    in_sem, out_sem = take(2)
    exchange_sems = [take(2) for _ in range(4)]
    gather_sems = [take(5) for _ in range(2)]
    scatter_sems = [take(5) for _ in range(2)]

    gathers = [Gather(True, up_all, *gather_sems[0]), Gather(False, down_all, *gather_sems[1])]
    homes = (frames, kernel, up_all.at[gathers[0].here()], down_all.at[gathers[1].here()], cot)
    own = [pltpu.make_async_copy(a, b, in_sem.at[i]) for i, (a, b) in enumerate(zip(inputs, homes))]
    for i in (4, 2, 3, 0, 1):
        own[i].start()
    announce(count)

    def write(i, ref):
        copy = pltpu.make_async_copy(ref, outputs[i], out_sem.at[i])
        copy.start()
        written.append(copy)

    written = []
    to_slopes = Exchange(count, send_slopes, recv_slopes, *exchange_sems[0])
    to_rows = Exchange(count, send_rows, recv_rows, *exchange_sems[1])
    to_out = Exchange(count, back_out, recv_out, *exchange_sems[2])
    to_grad = Exchange(count, back_grad, recv_grad, *exchange_sems[3])
    scatters = [
        Scatter(True, up_parts, *up_room, *scatter_sems[0]),
        Scatter(False, down_parts, *down_room, *scatter_sems[1]),
    ]
    sides = [(slopes, rows_in), (hidden, slopes_in)]

    route_places(routes, ranks, place)
    live_columns(length, gates, mask, gate)
    own[4].wait()
    pack_slopes(cot, gate, place, send_slopes)
    enter(count)
    to_slopes.start()
    for i in (2, 3):
        own[i].wait()
    for gather in gathers:
        gather.start()
    for i in (0, 1):
        own[i].wait()
    front_norm(frames, mask, hat1, inv1, pad)
    depthwise(pad, kernel, conv, False)
    front_residual(frames, conv, res, hat2, inv2, normed)
    pack_rows(normed, place, send_rows)
    to_rows.start()

    for gather in gathers:
        gather.relay_near()
    for gather in gathers:
        gather.relay_row(0)
    for gather in gathers:
        gather.relay_far()
    for k in (1, 2, 3):
        for gather in gathers:
            gather.relay_row(k)
    turn_places(ranks, turned)
    to_slopes.arrive()
    unpack(recv_slopes, slopes_in)
    for k in range(SIDE):
        for gather in gathers:
            gather.end_row(k)
    hidden_grads(slopes_in, down_all, wide)
    to_rows.arrive()
    unpack(recv_rows, rows_in)
    hidden_units(rows_in, up_all, wide, hidden, slopes)
    project(slopes, up_all, row_sum)
    pack(row_sum, back_grad)
    to_grad.start()

    for scatter, (left, right) in zip(scatters, sides):
        weight_grads(scatter, 2, left, right)
        for i in range(SIDE):
            scatter.send_far(i)
    project(hidden, down_all, row_sum)
    pack(row_sum, back_out)
    to_out.start()
    for step in (1, -1):
        for scatter, (left, right) in zip(scatters, sides):
            weight_grads(scatter, step, left, right)
    for i in range(SIDE):
        for scatter in scatters:
            for d in (0, 1):
                scatter.send_near(d, i)
    for scatter, (left, right) in zip(scatters, sides):
        weight_grads(scatter, 0, left, right)
    for scatter in scatters:
        scatter.keep(0)
        scatter.send_far_last()
    for d in (0, 1):
        for scatter in scatters:
            scatter.keep(1 + d)
            scatter.send_near_last(d)

    to_grad.arrive()
    back_slopes(recv_grad, turned, normed_grad)
    back_residual(cot, hat2, inv2, conv, normed_grad, pad)
    depthwise(pad, kernel, first_grad, True)
    back_frames(first_grad, mask, hat1, inv1, normed_grad, frame_grad)
    write(1, frame_grad)
    for i, (scatter, out) in enumerate(zip(scatters, (up_grad, down_grad))):
        scatter.last(out)
        write(2 + i, out)
    to_out.arrive()
    back_mix(recv_out, turned, gate, res, block_out)
    write(0, block_out)

    for exchange in (to_slopes, to_rows, to_out, to_grad):
        exchange.finish()
    for ring, blocks in zip(gathers + scatters, (up_all, down_all, up_parts, down_parts)):
        ring.finish(blocks)
    for copy in written:
        copy.wait()


def hand_over(*refs):
    n = (len(refs) - 2) // 3
    inputs, outputs, rooms = refs[:n], refs[n : 2 * n], refs[2 * n : 3 * n]
    in_sem, out_sem = refs[3 * n :]
    reads = [pltpu.make_async_copy(inputs[i], rooms[i], in_sem.at[i]) for i in range(n)]
    writes = [pltpu.make_async_copy(rooms[i], outputs[i], out_sem.at[i]) for i in range(n)]
    for copy in reads:
        copy.start()
    for i in range(n):
        reads[i].wait()
        writes[i].start()
    for copy in writes:
        copy.wait()


def on_device(frames, lengths, routes, gate_weights, kernel, up_weight, down_weight, cotangent):
    experts = lax.axis_size("ep")
    reps = lax.axis_size("rep")
    count, width = frames.shape
    unit = up_weight.shape[1]
    rows = experts * CAP
    half = width // 2
    vmem = pltpu.VMEM
    packed = vmem((experts, 2 * CAP, half), BF16)
    grid32 = vmem((count, width), F32)
    column = vmem((count, 1), F32)
    weights = vmem((reps, unit, width), BF16)
    room = [
        vmem((2, SIDE, unit // 2, width), BF16),
        vmem((2, SIDE, unit, width), BF16),
        vmem((3, unit, width), BF16),
        vmem((2, unit // 2, width), BF16),
        vmem((2, unit, width), BF16),
    ]
    narrow = vmem((count, width), BF16)
    scratch = [weights, weights]
    scratch += [narrow, vmem(kernel.shape, F32), narrow]
    scratch += [narrow, narrow, vmem((unit, width), F32), vmem((unit, width), F32)]
    scratch += [vmem((2, count), F32), vmem((2 * rows, 4 * count), BF16)]
    scratch += [vmem((4, count, 2 * rows), BF16), column, vmem((2, count, 1), F32)]
    scratch += [narrow, grid32, column, vmem((count + 2 * EDGE, width), F32)]
    scratch += [grid32, grid32, grid32, column]
    scratch += [packed] * 8
    scratch += [vmem((rows, width), BF16)] * 2
    scratch += [vmem((reps, rows, unit), F32)]
    scratch += [vmem((rows, reps * unit), BF16)] * 2
    scratch += [vmem((rows, width), F32)]
    scratch += [grid32, grid32, weights, weights] + room + room
    scratch += [DMA((5,)), DMA((4,))]
    scratch += [DMA((1,))] * 8
    scratch += [DMA((1,)), DMA((2,)), DMA((2,)), DMA((2, SIDE)), DMA((2, SIDE))] * 2
    scratch += [DMA((1,)), DMA((2, SIDE)), DMA((2, SIDE)), DMA((2,)), DMA((2,))] * 2

    in_vmem = pl.BlockSpec(memory_space=pltpu.VMEM)
    anywhere = pl.BlockSpec(memory_space=pl.ANY)
    shapes = [jax.ShapeDtypeStruct((count, width), BF16)] * 2
    shapes += [jax.ShapeDtypeStruct((unit, width), F32)] * 2
    results = pl.pallas_call(
        functools.partial(block_kernel, experts),
        out_shape=shapes,
        in_specs=[in_vmem] * 3 + [anywhere] * 5,
        out_specs=[anywhere] * 4,
        scratch_shapes=scratch,
        compiler_params=pltpu.CompilerParams(
            collective_id=0, has_side_effects=True, vmem_limit_bytes=58 << 20
        ),
        cost_estimate=pl.CostEstimate(
            flops=12 * rows * reps * unit * width, bytes_accessed=8 << 20, transcendentals=0
        ),
    )(
        lengths.reshape(1, 1),
        routes.T,
        gate_weights.T,
        frames,
        kernel,
        up_weight[0],
        down_weight[0],
        cotangent,
    )
    block_out, frame_grad, up_grad, down_grad = pl.pallas_call(
        hand_over,
        out_shape=shapes,
        in_specs=[anywhere] * 4,
        out_specs=[anywhere] * 4,
        scratch_shapes=[vmem(s.shape, s.dtype) for s in shapes] + [DMA((4,)), DMA((4,))],
        compiler_params=pltpu.CompilerParams(vmem_limit_bytes=58 << 20),
    )(*results)
    return block_out, frame_grad, up_grad[None], down_grad[None]


def solution(mesh):
    in_specs = (
        P(("ep", "rep"), None),
        P(("ep", "rep")),
        P(("ep", "rep"), None),
        P(("ep", "rep"), None),
        P(),
        P("ep", "rep", None),
        P("ep", "rep", None),
        P(("ep", "rep"), None),
    )
    out_specs = (
        P(("ep", "rep"), None),
        P(("ep", "rep"), None),
        P("ep", "rep", None),
        P("ep", "rep", None),
    )
    return jax.shard_map(
        on_device, mesh=mesh, in_specs=in_specs, out_specs=out_specs, check_vma=False
    )
```

time: 141 us -> 125 us (0.89)
  Pallas kernels: 132 us -> 123 us
  local copies, waits for them, and re-layouts: 5.99 us -> 0 us
    pallas_call x1 -> x2, Pallas kernels: 132 us -> 123 us  [the longest x1 121 us: on_device(): pl.pallas_call(functools.partial(block_kernel, experts), out_shape=shapes...]
    unnamed x16 -> x0, local copies, waits for them, and re-layouts: 5.99 us -> none
where the time goes in v2:
time: 125 us
  Pallas kernels  123 us (98%)
  between operations  1.29 us (1%)
    pallas_call x1, Pallas kernels, on_device(): pl.pallas_call(functools.partial(block_kernel, experts), out_shape=shapes...  121 us

profile of v2, /device:TPU:1, one launch (start us, length us, event | category | flops | bytes accessed | tf_op | source)
XLA Modules:
  0.0 124.7 jit_solution(11968327782425692085)
XLA Ops:
  1.3 121.2 %shard_map.111 = (bf16[128,1024]{1,0:T(8,128)(2,1)}, bf16[128,1024]{1,0:T(8,128)(2,1)}, f32[128,1024]{1,0:T(8,128)}, f32[128,1024]{1,0:T(8,128)}) custom-call(s32[1,1]{1,0:T(1,128)} %bitcast.7.refs_0_, s32[2,128]{1,0:T(2,128)} %bitcast.12, f32[2,128]{1,0:T(2,128)} %bitcast.13, bf16[128,1024]{1,0:T(8,128)(2,1)} %refs_3_.1, f32[31,1024]{1,0:T(8,128)} %refs_4_.1, ...), custom_call_target="tpu_custom_call" | custom-call | flops 6442450944 | bytes 8388608 | tf_op jit(solution)/shard_map/pallas_call | solution.py:710
  122.5 2.2 %shard_map.112 = (bf16[128,1024]{1,0:T(8,128)(2,1)}, bf16[128,1024]{1,0:T(8,128)(2,1)}, f32[128,1024]{1,0:T(8,128)}, f32[128,1024]{1,0:T(8,128)}) custom-call(bf16[128,1024]{1,0:T(8,128)(2,1)} %get-tuple-element.12.refs_0_, bf16[128,1024]{1,0:T(8,128)(2,1)} %get-tuple-element.13.refs_1_, f32[128,1024]{1,0:T(8,128)} %get-tuple-element.14.refs_2_, ...), custom_call_target="tpu_custom_call" | custom-call | tf_op jit(solution)/shard_map/pallas_call | solution.py:732

commit v3 on v2

--- a/solution.py
+++ b/solution.py
@@ -458,16 +458,17 @@
     return pair.reshape(2 * pair.shape[1], pair.shape[2])
 
 
-def hidden_grads(slopes_in_ref, down_ref, wide_ref):
+def hidden_grads(slopes_in_ref, down_ref, wide_ref, side):
     unit = down_ref.shape[1]
 
-    def run(j, carry):
+    def run(i, carry):
+        j = (SIDE // 2) * i + side
         grads = contract_last(slopes_in_ref[...], weight_rows(down_ref, j))
         wide_ref[2 * j] = grads[:, :unit]
         wide_ref[2 * j + 1] = grads[:, unit:]
         return carry
 
-    lax.fori_loop(0, down_ref.shape[0] // 2, run, 0)
+    lax.fori_loop(0, SIDE, run, 0, unroll=True)
 
 
 def hidden_units(rows_ref, up_ref, wide_ref, hidden_ref, slopes_ref):
@@ -488,7 +489,7 @@
             slopes_ref[:, at] = slopes.astype(BF16)
         return carry
 
-    lax.fori_loop(0, up_ref.shape[0] // 2, run, 0)
+    lax.fori_loop(0, up_ref.shape[0] // 2, run, 0, unroll=True)
 
 
 def project(left_ref, weight_ref, sum_ref):
@@ -500,7 +501,7 @@
         sum_ref[:, at] = jnp.dot(left_ref[...], right, preferred_element_type=F32)
         return carry
 
-    lax.fori_loop(0, sum_ref.shape[1] // tile, run, 0)
+    lax.fori_loop(0, sum_ref.shape[1] // tile, run, 0, unroll=True)
 
 
 def weight_grads(scatter, step, left_ref, right_ref):
@@ -514,7 +515,7 @@
         scatter.parts[pl.ds(block, 2)] = grads.reshape(2, unit, -1)
         return carry
 
-    lax.fori_loop(0, SIDE // 2, run, 0)
+    lax.fori_loop(0, SIDE // 2, run, 0, unroll=True)
 
 
 def block_kernel(count, *refs):
@@ -594,10 +595,12 @@
     turn_places(ranks, turned)
     to_slopes.arrive()
     unpack(recv_slopes, slopes_in)
+    near_side = lax.div(gathers[1].second, SIDE // 2)
+    hidden_grads(slopes_in, down_all, wide, near_side)
     for k in range(SIDE):
         for gather in gathers:
             gather.end_row(k)
-    hidden_grads(slopes_in, down_all, wide)
+    hidden_grads(slopes_in, down_all, wide, 1 - near_side)
     to_rows.arrive()
     unpack(recv_rows, rows_in)
     hidden_units(rows_in, up_all, wide, hidden, slopes)
@@ -605,29 +608,38 @@
     pack(row_sum, back_grad)
     to_grad.start()
 
-    for scatter, (left, right) in zip(scatters, sides):
-        weight_grads(scatter, 2, left, right)
-        for i in range(SIDE):
-            scatter.send_far(i)
+    def each(step):
+        for scatter in scatters:
+            step(scatter)
+
+    def both_near(i):
+        for d in (0, 1):
+            each(lambda scatter: scatter.send_near(d, i))
+
+    def all_grads(step):
+        for scatter, (left, right) in zip(scatters, sides):
+            weight_grads(scatter, step, left, right)
+
+    all_grads(2)
+    each(lambda scatter: scatter.send_far(0))
+    each(lambda scatter: scatter.send_far(1))
     project(hidden, down_all, row_sum)
     pack(row_sum, back_out)
     to_out.start()
-    for step in (1, -1):
-        for scatter, (left, right) in zip(scatters, sides):
-            weight_grads(scatter, step, left, right)
-    for i in range(SIDE):
-        for scatter in scatters:
-            for d in (0, 1):
-                scatter.send_near(d, i)
-    for scatter, (left, right) in zip(scatters, sides):
-        weight_grads(scatter, 0, left, right)
-    for scatter in scatters:
-        scatter.keep(0)
-        scatter.send_far_last()
+    all_grads(1)
+    all_grads(-1)
+    each(lambda scatter: scatter.send_far(2))
+    both_near(0)
+    each(lambda scatter: scatter.send_far(3))
+    both_near(1)
+    all_grads(0)
+    both_near(2)
+    each(lambda scatter: scatter.keep(0))
+    each(lambda scatter: scatter.send_far_last())
+    both_near(3)
     for d in (0, 1):
-        for scatter in scatters:
-            scatter.keep(1 + d)
-            scatter.send_near_last(d)
+        each(lambda scatter: scatter.keep(1 + d))
+        each(lambda scatter: scatter.send_near_last(d))
 
     to_grad.arrive()
     back_slopes(recv_grad, turned, normed_grad)

time: 125 us -> 119 us (0.952)
  Pallas kernels: 123 us -> 118 us
    pallas_call x1, Pallas kernels: 121 us -> 116 us  [on_device(): pl.pallas_call(functools.partial(block_kernel, experts), out_shape=shapes...]
where the time goes in v3:
time: 119 us
  Pallas kernels  118 us (99%)
  between operations  1.29 us (1%)
    pallas_call x1, Pallas kernels, on_device(): pl.pallas_call(functools.partial(block_kernel, experts), out_shape=shapes...  116 us

profile of v3, /device:TPU:1, one launch (start us, length us, event | category | flops | bytes accessed | tf_op | source)
XLA Modules:
  0.0 119.2 jit_solution(8927766607184879400)
XLA Ops:
  1.3 115.7 %shard_map.111 = (bf16[128,1024]{1,0:T(8,128)(2,1)}, bf16[128,1024]{1,0:T(8,128)(2,1)}, f32[128,1024]{1,0:T(8,128)}, f32[128,1024]{1,0:T(8,128)}) custom-call(s32[1,1]{1,0:T(1,128)} %bitcast.7.refs_0_, s32[2,128]{1,0:T(2,128)} %bitcast.12, f32[2,128]{1,0:T(2,128)} %bitcast.13, bf16[128,1024]{1,0:T(8,128)(2,1)} %refs_3_.1, f32[31,1024]{1,0:T(8,128)} %refs_4_.1, ...), custom_call_target="tpu_custom_call" | custom-call | flops 6442450944 | bytes 8388608 | tf_op jit(solution)/shard_map/pallas_call | solution.py:722
  117.0 2.2 %shard_map.112 = (bf16[128,1024]{1,0:T(8,128)(2,1)}, bf16[128,1024]{1,0:T(8,128)(2,1)}, f32[128,1024]{1,0:T(8,128)}, f32[128,1024]{1,0:T(8,128)}) custom-call(bf16[128,1024]{1,0:T(8,128)(2,1)} %get-tuple-element.12.refs_0_, bf16[128,1024]{1,0:T(8,128)(2,1)} %get-tuple-element.13.refs_1_, f32[128,1024]{1,0:T(8,128)} %get-tuple-element.14.refs_2_, ...), custom_call_target="tpu_custom_call" | custom-call | tf_op jit(solution)/shard_map/pallas_call | solution.py:744

commit v4 on v3

--- a/solution.py
+++ b/solution.py
@@ -524,11 +524,10 @@
     def take(n):
         return [next(names) for _ in range(n)]
 
-    length, routes, gates = take(3)
-    inputs, outputs = take(5), take(4)
+    inputs = take(8)
+    block_out, frame_grad, up_grad, down_grad = take(4)
     up_all, down_all = take(2)
-    frames, kernel, cot = take(3)
-    block_out, frame_grad, up_grad, down_grad = take(4)
+    length, routes, gates, frames, kernel, cot = take(6)
     ranks, place, turned, mask, gate = take(5)
     normed, hat1, inv1, pad, conv, res, hat2, inv2 = take(8)
     send_slopes, send_rows, recv_slopes, recv_rows = take(4)
@@ -537,24 +536,19 @@
     normed_grad, first_grad = take(2)
     up_parts, down_parts = take(2)
     up_room, down_room = take(5), take(5)
-    in_sem, out_sem = take(2)
+    (in_sem,) = take(1)
     exchange_sems = [take(2) for _ in range(4)]
     gather_sems = [take(5) for _ in range(2)]
     scatter_sems = [take(5) for _ in range(2)]
 
     gathers = [Gather(True, up_all, *gather_sems[0]), Gather(False, down_all, *gather_sems[1])]
-    homes = (frames, kernel, up_all.at[gathers[0].here()], down_all.at[gathers[1].here()], cot)
+    homes = (length, routes, gates, frames, kernel)
+    homes += (up_all.at[gathers[0].here()], down_all.at[gathers[1].here()], cot)
     own = [pltpu.make_async_copy(a, b, in_sem.at[i]) for i, (a, b) in enumerate(zip(inputs, homes))]
-    for i in (4, 2, 3, 0, 1):
+    announce(count)
+    for i in (1, 0, 2, 7, 5, 6, 3, 4):
         own[i].start()
-    announce(count)
-
-    def write(i, ref):
-        copy = pltpu.make_async_copy(ref, outputs[i], out_sem.at[i])
-        copy.start()
-        written.append(copy)
-
-    written = []
+
     to_slopes = Exchange(count, send_slopes, recv_slopes, *exchange_sems[0])
     to_rows = Exchange(count, send_rows, recv_rows, *exchange_sems[1])
     to_out = Exchange(count, back_out, recv_out, *exchange_sems[2])
@@ -565,17 +559,20 @@
     ]
     sides = [(slopes, rows_in), (hidden, slopes_in)]
 
+    own[1].wait()
     route_places(routes, ranks, place)
+    own[0].wait()
+    own[2].wait()
     live_columns(length, gates, mask, gate)
-    own[4].wait()
+    own[7].wait()
     pack_slopes(cot, gate, place, send_slopes)
     enter(count)
     to_slopes.start()
-    for i in (2, 3):
+    for i in (5, 6):
         own[i].wait()
     for gather in gathers:
         gather.start()
-    for i in (0, 1):
+    for i in (3, 4):
         own[i].wait()
     front_norm(frames, mask, hat1, inv1, pad)
     depthwise(pad, kernel, conv, False)
@@ -646,34 +643,23 @@
     back_residual(cot, hat2, inv2, conv, normed_grad, pad)
     depthwise(pad, kernel, first_grad, True)
     back_frames(first_grad, mask, hat1, inv1, normed_grad, frame_grad)
-    write(1, frame_grad)
-    for i, (scatter, out) in enumerate(zip(scatters, (up_grad, down_grad))):
+    for scatter, out in zip(scatters, (up_grad, down_grad)):
         scatter.last(out)
-        write(2 + i, out)
     to_out.arrive()
     back_mix(recv_out, turned, gate, res, block_out)
-    write(0, block_out)
 
     for exchange in (to_slopes, to_rows, to_out, to_grad):
         exchange.finish()
     for ring, blocks in zip(gathers + scatters, (up_all, down_all, up_parts, down_parts)):
         ring.finish(blocks)
-    for copy in written:
-        copy.wait()
 
 
 def hand_over(*refs):
-    n = (len(refs) - 2) // 3
-    inputs, outputs, rooms = refs[:n], refs[n : 2 * n], refs[2 * n : 3 * n]
-    in_sem, out_sem = refs[3 * n :]
-    reads = [pltpu.make_async_copy(inputs[i], rooms[i], in_sem.at[i]) for i in range(n)]
-    writes = [pltpu.make_async_copy(rooms[i], outputs[i], out_sem.at[i]) for i in range(n)]
-    for copy in reads:
+    n = (len(refs) - 1) // 2
+    copies = [pltpu.make_async_copy(refs[i], refs[n + i], refs[-1].at[i]) for i in range(n)]
+    for copy in copies:
         copy.start()
-    for i in range(n):
-        reads[i].wait()
-        writes[i].start()
-    for copy in writes:
+    for copy in copies:
         copy.wait()
 
 
@@ -698,8 +684,8 @@
     ]
     narrow = vmem((count, width), BF16)
     scratch = [weights, weights]
+    scratch += [vmem((1, 1), jnp.int32), vmem((2, count), jnp.int32), vmem((2, count), F32)]
     scratch += [narrow, vmem(kernel.shape, F32), narrow]
-    scratch += [narrow, narrow, vmem((unit, width), F32), vmem((unit, width), F32)]
     scratch += [vmem((2, count), F32), vmem((2 * rows, 4 * count), BF16)]
     scratch += [vmem((4, count, 2 * rows), BF16), column, vmem((2, count, 1), F32)]
     scratch += [narrow, grid32, column, vmem((count + 2 * EDGE, width), F32)]
@@ -710,20 +696,20 @@
     scratch += [vmem((rows, reps * unit), BF16)] * 2
     scratch += [vmem((rows, width), F32)]
     scratch += [grid32, grid32, weights, weights] + room + room
-    scratch += [DMA((5,)), DMA((4,))]
+    scratch += [DMA((8,))]
     scratch += [DMA((1,))] * 8
     scratch += [DMA((1,)), DMA((2,)), DMA((2,)), DMA((2, SIDE)), DMA((2, SIDE))] * 2
     scratch += [DMA((1,)), DMA((2, SIDE)), DMA((2, SIDE)), DMA((2,)), DMA((2,))] * 2
 
+    anywhere = pl.BlockSpec(memory_space=pl.ANY)
     in_vmem = pl.BlockSpec(memory_space=pltpu.VMEM)
-    anywhere = pl.BlockSpec(memory_space=pl.ANY)
     shapes = [jax.ShapeDtypeStruct((count, width), BF16)] * 2
     shapes += [jax.ShapeDtypeStruct((unit, width), F32)] * 2
     results = pl.pallas_call(
         functools.partial(block_kernel, experts),
-        out_shape=shapes,
-        in_specs=[in_vmem] * 3 + [anywhere] * 5,
-        out_specs=[anywhere] * 4,
+        out_shape=[vmem(s.shape, s.dtype) for s in shapes],
+        in_specs=[anywhere] * 8,
+        out_specs=[in_vmem] * 4,
         scratch_shapes=scratch,
         compiler_params=pltpu.CompilerParams(
             collective_id=0, has_side_effects=True, vmem_limit_bytes=58 << 20
@@ -746,8 +732,8 @@
         out_shape=shapes,
         in_specs=[anywhere] * 4,
         out_specs=[anywhere] * 4,
-        scratch_shapes=[vmem(s.shape, s.dtype) for s in shapes] + [DMA((4,)), DMA((4,))],
-        compiler_params=pltpu.CompilerParams(vmem_limit_bytes=58 << 20),
+        scratch_shapes=[DMA((4,))],
+        compiler_params=pltpu.CompilerParams(vmem_limit_bytes=4 << 20),
     )(*results)
     return block_out, frame_grad, up_grad[None], down_grad[None]
 

time: 119 us -> 117 us (0.983)
  Pallas kernels: 118 us -> 116 us
    pallas_call x1, Pallas kernels: 116 us -> 114 us  [on_device(): pl.pallas_call(functools.partial(block_kernel, experts), out_shape=[vmem(...]
where the time goes in v4:
time: 117 us
  Pallas kernels  116 us (99%)
  between operations  1.29 us (1%)
    pallas_call x1, Pallas kernels, on_device(): pl.pallas_call(functools.partial(block_kernel, experts), out_shape=[vmem(...  114 us

profile of v4, /device:TPU:1, one launch (start us, length us, event | category | flops | bytes accessed | tf_op | source)
XLA Modules:
  0.0 116.9 jit_solution(18052825875175764062)
XLA Ops:
  1.3 114.4 %shard_map.111 = (bf16[128,1024]{1,0:T(8,128)(2,1)S(1)}, bf16[128,1024]{1,0:T(8,128)(2,1)S(1)}, f32[128,1024]{1,0:T(8,128)S(1)}, f32[128,1024]{1,0:T(8,128)S(1)}) custom-call(s32[1,1]{1,0:T(1,128)} %bitcast.7.refs_0_, s32[2,128]{1,0:T(2,128)} %bitcast.12, f32[2,128]{1,0:T(2,128)} %bitcast.13, bf16[128,1024]{1,0:T(8,128)(2,1)} %refs_3_.1, ...), custom_call_target="tpu_custom_call" | custom-call | flops 6442450944 | bytes 8388608 | tf_op jit(solution)/shard_map/pallas_call | solution.py:708
  115.7 1.2 %shard_map.112 = (bf16[128,1024]{1,0:T(8,128)(2,1)}, bf16[128,1024]{1,0:T(8,128)(2,1)}, f32[128,1024]{1,0:T(8,128)}, f32[128,1024]{1,0:T(8,128)}) custom-call(bf16[128,1024]{1,0:T(8,128)(2,1)S(1)} %get-tuple-element.12.refs_0_, bf16[128,1024]{1,0:T(8,128)(2,1)S(1)} %get-tuple-element.13.refs_1_, f32[128,1024]{1,0:T(8,128)S(1)} %get-tuple-element.14.refs_2_, ...), custom_call_target="tpu_custom_call" | custom-call | tf_op jit(solution)/shard_map/pallas_call | solution.py:730

commit v5 on v4

--- a/solution.py
+++ b/solution.py
@@ -439,20 +439,6 @@
     lax.fori_loop(0, count // step, run, 0)
 
 
-def pack(rows_ref, packed_ref):
-    count, _, half = packed_ref.shape
-    step = 4
-
-    def run(i, carry):
-        block = rows_ref[pl.ds(pl.multiple_of(i * step * CAP, step * CAP), step * CAP)]
-        block = block.reshape(step, CAP, 2 * half)
-        both = jnp.concatenate([block[:, :, :half], block[:, :, half:]], axis=1)
-        packed_ref[pl.ds(i * step, step)] = both.astype(BF16)
-        return carry
-
-    lax.fori_loop(0, count // step, run, 0)
-
-
 def weight_rows(weight_ref, j):
     pair = weight_ref[pl.ds(2 * j, 2)]
     return pair.reshape(2 * pair.shape[1], pair.shape[2])
@@ -492,16 +478,22 @@
     lax.fori_loop(0, up_ref.shape[0] // 2, run, 0, unroll=True)
 
 
-def project(left_ref, weight_ref, sum_ref):
+def project(left_ref, weight_ref, packed_ref):
+    count, _, half = packed_ref.shape
     tile = 256
 
     def run(j, carry):
+        parts = []
+        for h in range(2):
+            at = pl.ds(pl.multiple_of(h * half + j * tile, tile), tile)
+            right = weight_ref[:, :, at].reshape(-1, tile)
+            part = jnp.dot(left_ref[...], right, preferred_element_type=F32)
+            parts.append(part.reshape(count, CAP, tile))
         at = pl.ds(pl.multiple_of(j * tile, tile), tile)
-        right = weight_ref[:, :, at].reshape(-1, tile)
-        sum_ref[:, at] = jnp.dot(left_ref[...], right, preferred_element_type=F32)
+        packed_ref[:, :, at] = jnp.concatenate(parts, axis=1).astype(BF16)
         return carry
 
-    lax.fori_loop(0, sum_ref.shape[1] // tile, run, 0, unroll=True)
+    lax.fori_loop(0, half // tile, run, 0, unroll=True)
 
 
 def weight_grads(scatter, step, left_ref, right_ref):
@@ -532,7 +524,7 @@
     normed, hat1, inv1, pad, conv, res, hat2, inv2 = take(8)
     send_slopes, send_rows, recv_slopes, recv_rows = take(4)
     back_out, back_grad, recv_out, recv_grad = take(4)
-    slopes_in, rows_in, wide, hidden, slopes, row_sum = take(6)
+    slopes_in, rows_in, wide, hidden, slopes = take(5)
     normed_grad, first_grad = take(2)
     up_parts, down_parts = take(2)
     up_room, down_room = take(5), take(5)
@@ -601,8 +593,7 @@
     to_rows.arrive()
     unpack(recv_rows, rows_in)
     hidden_units(rows_in, up_all, wide, hidden, slopes)
-    project(slopes, up_all, row_sum)
-    pack(row_sum, back_grad)
+    project(slopes, up_all, back_grad)
     to_grad.start()
 
     def each(step):
@@ -620,8 +611,7 @@
     all_grads(2)
     each(lambda scatter: scatter.send_far(0))
     each(lambda scatter: scatter.send_far(1))
-    project(hidden, down_all, row_sum)
-    pack(row_sum, back_out)
+    project(hidden, down_all, back_out)
     to_out.start()
     all_grads(1)
     all_grads(-1)
@@ -694,7 +684,6 @@
     scratch += [vmem((rows, width), BF16)] * 2
     scratch += [vmem((reps, rows, unit), F32)]
     scratch += [vmem((rows, reps * unit), BF16)] * 2
-    scratch += [vmem((rows, width), F32)]
     scratch += [grid32, grid32, weights, weights] + room + room
     scratch += [DMA((8,))]
     scratch += [DMA((1,))] * 8

time: 117 us -> 117 us (level)
  no operation moved by 1% of the time
where the time goes in v5:
time: 117 us
  Pallas kernels  116 us (99%)
  between operations  1.29 us (1%)
    pallas_call x1, Pallas kernels, on_device(): pl.pallas_call(functools.partial(block_kernel, experts), out_shape=[vmem(...  114 us

profile of v5, /device:TPU:1, one launch (start us, length us, event | category | flops | bytes accessed | tf_op | source)
XLA Modules:
  0.0 116.8 jit_solution(4847338566015311015)
XLA Ops:
  1.3 114.3 %shard_map.111 = (bf16[128,1024]{1,0:T(8,128)(2,1)S(1)}, bf16[128,1024]{1,0:T(8,128)(2,1)S(1)}, f32[128,1024]{1,0:T(8,128)S(1)}, f32[128,1024]{1,0:T(8,128)S(1)}) custom-call(s32[1,1]{1,0:T(1,128)} %bitcast.7.refs_0_, s32[2,128]{1,0:T(2,128)} %bitcast.12, f32[2,128]{1,0:T(2,128)} %bitcast.13, bf16[128,1024]{1,0:T(8,128)(2,1)} %refs_3_.1, ...), custom_call_target="tpu_custom_call" | custom-call | flops 6442450944 | bytes 8388608 | tf_op jit(solution)/shard_map/pallas_call | solution.py:697
  115.6 1.2 %shard_map.112 = (bf16[128,1024]{1,0:T(8,128)(2,1)}, bf16[128,1024]{1,0:T(8,128)(2,1)}, f32[128,1024]{1,0:T(8,128)}, f32[128,1024]{1,0:T(8,128)}) custom-call(bf16[128,1024]{1,0:T(8,128)(2,1)S(1)} %get-tuple-element.12.refs_0_, bf16[128,1024]{1,0:T(8,128)(2,1)S(1)} %get-tuple-element.13.refs_1_, f32[128,1024]{1,0:T(8,128)S(1)} %get-tuple-element.14.refs_2_, ...), custom_call_target="tpu_custom_call" | custom-call | tf_op jit(solution)/shard_map/pallas_call | solution.py:719
